TPU v7x, 256 devices: a whole 4x4x8 slice. The times are simulated.
256 devices in a mesh: tile: 64 (over x, y, z_hi), lev: 4 (over z_lo, core).
Axes of the slice: x: 4, y: 4, z: 8 (z_hi: 4, z_lo: 2; z = z_hi * 2 + z_lo), core: 2. Of those that a mesh axis runs over, the one named last changes fastest.
Arguments:
- state: float32 [4, 32, 256, 128], P(None, 'lev', 'tile'), may hold values from -6 to 6
- coef_x: float32 [32, 256, 128], P('lev', 'tile'), may hold values from 0.2 to 0.6
- coef_y: float32 [32, 256, 128], P('lev', 'tile'), may hold values from 0.2 to 0.6
- coef_z: float32 [32, 256, 128], P('lev', 'tile'), may hold values from 0.2 to 0.6
- slope: float32 [32, 256, 128], P('lev', 'tile'), may hold values from -0.3 to 0.3
- compress: float32 [32, 256, 128], P('lev', 'tile'), may hold values from 0.2 to 0.6
- ground: int32 [256, 128], P('tile'), may hold values from 0 to 8
- w_in: bfloat16 [4, 512], replicated, may hold values from -3 to 3
- level_table: float32 [32, 512], replicated, may hold values from -6 to 6
- gain_attn: float32 [512], replicated, may hold values from 0.1 to 1.9
- w_query: bfloat16 [512, 512], replicated, may hold values from -0.25 to 0.25
- w_key: bfloat16 [512, 512], replicated, may hold values from -0.25 to 0.25
- w_value: bfloat16 [512, 512], replicated, may hold values from -0.25 to 0.25
- w_mix: bfloat16 [512, 512], replicated, may hold values from -0.25 to 0.25
- temper: float32 [8], replicated, may hold values from 0.5 to 64, as said below
- gain_head: float32 [512], replicated, may hold values from 0.1 to 1.9
- w_tend: bfloat16 [512, 4], replicated, may hold values from -0.25 to 0.25
Outputs:
- updated: float32 [4, 32, 256, 128], P(None, 'lev', 'tile')
Inputs may be any that keep to these rules, and one draw needn't show every extreme that they name: `temper`: positive score scales of the heads.
All inputs are finite; a program needn't handle non-finite values.
Results may differ from a plain program's by a relative error of at most 0.024.
Values may be sent and summed in bfloat16 or wider, within the bound.
A program may use at most 128 MiB of HBM per device.

v0:
```python
import math

import jax
import jax.numpy as jnp
from jax import lax
from jax.sharding import PartitionSpec as P

SUBSTEPS = 3


EPS = 1e-06


def from_behind(value, axis, steps):
    count = lax.axis_size(axis)
    leading, last = (max(0, -steps), min(count, count - steps))
    return lax.ppermute(value, axis, [(source, source + steps) for source in range(leading, last)])


def with_halo(block, sides, width):
    for axis, dim in sides:
        count = lax.axis_size(axis)
        forward = [(i, i + 1) for i in range(count - 1)]
        backward = [(target, source) for source, target in forward]
        low = lax.ppermute(
            lax.slice_in_dim(block, block.shape[dim] - width, None, axis=dim), axis, forward
        )
        high = lax.ppermute(lax.slice_in_dim(block, 0, width, axis=dim), axis, backward)
        block = jnp.concatenate([low, block, high], axis=dim)
    return block


def acoustic(padded, metrics, coef_y, compress):
    pressure = padded[0]
    east_wind = padded[1]
    north_wind = padded[2]
    upward = padded[3]
    grad_x = metrics[0]
    slope_pad = metrics[1]
    grad_z = metrics[2]
    inner_k = pressure[1:-1]
    east_new = (
        east_wind[1:-1, :-1]
        - grad_x[1:-1, :-1] * (inner_k[:, 1:] - inner_k[:, :-1])
        - 0.5 * slope_pad[1:-1, :-1] * (pressure[2:, :-1] - pressure[:-2, :-1])
    )
    inner_x = pressure[:, 1:-1]
    upward_new = upward[:-1, 1:-1] - grad_z[:-1, 1:-1] * (inner_x[1:] - inner_x[:-1])
    centre = pressure[1:-1, 1:-1]
    north_new = north_wind[1:-1, 1:-1] - coef_y * (jnp.roll(centre, -1, axis=2) - centre)
    divergence = (
        east_new[:, 1:]
        - east_new[:, :-1]
        + (north_new - jnp.roll(north_new, 1, axis=2))
        + (upward_new[1:] - upward_new[:-1])
    )
    pressure_new = centre - compress * divergence
    return jnp.stack([pressure_new, east_new[:, 1:], north_new, upward_new[1:]])


def multiply(pattern, first_op, second_op):
    return jnp.einsum(pattern, first_op, second_op, preferred_element_type=jnp.float32)


def rms_scale(values, over_dim):
    return values * lax.rsqrt(jnp.mean(values * values, axis=over_dim, keepdims=True) + EPS)


def embed(features, w_in, table_rows):
    summed = multiply("flc,fd->dlc", features, w_in) + jnp.transpose(table_rows)[:, :, None]
    return summed.astype(jnp.bfloat16)


def physics(
    embedded, ground_cols, gain_attn, w_query, w_key, w_value, w_mix, temper, gain_head, w_tend
):
    model_width, levels, columns = embedded.shape
    head_count = temper.shape[0]
    head_size = model_width // head_count
    stream = embedded.astype(jnp.float32)
    normed = (rms_scale(stream, 0) * gain_attn[:, None, None]).astype(jnp.bfloat16)

    def heads_of(weight):
        return multiply("dlc,de->elc", normed, weight).reshape(
            head_count, head_size, levels, columns
        )

    query_heads = rms_scale(heads_of(w_query), 1).astype(jnp.bfloat16)
    key_heads = rms_scale(heads_of(w_key), 1).astype(jnp.bfloat16)
    value_heads = heads_of(w_value).astype(jnp.bfloat16)
    scores = (
        multiply("hjlc,hjmc->hlmc", query_heads, key_heads)
        * (temper / math.sqrt(head_size))[:, None, None, None]
    )
    over_ground = jnp.arange(levels, dtype=jnp.int32)[:, None] >= ground_cols[None, :]
    scores = jnp.where(over_ground[None, None], scores, -1e30)
    peak = jnp.max(scores, axis=2, keepdims=True)
    weights = jnp.exp(scores - peak)
    probabilities = (weights / jnp.sum(weights, axis=2, keepdims=True)).astype(jnp.bfloat16)
    mixed_heads = multiply("hlmc,hjmc->hjlc", probabilities, value_heads).astype(jnp.bfloat16)
    mixed_heads = mixed_heads.reshape(model_width, levels, columns)
    stream = stream + multiply("dlc,de->elc", mixed_heads, w_mix)
    final_normed = (rms_scale(stream, 0) * gain_head[:, None, None]).astype(jnp.bfloat16)
    return multiply("dlc,df->flc", final_normed, w_tend)


def coefficient_rims(coef_x, slope, coef_z):
    levels, row_count, cells_y = coef_x.shape
    flat_pair = jnp.stack([coef_x, slope])
    below_rows = from_behind(flat_pair[:, :, row_count - 1 :, :], "tile", 1)
    pair_rows = jnp.concatenate(
        [below_rows, flat_pair, jnp.zeros((2, levels, 1, cells_y), jnp.float32)], axis=2
    )
    pair_full = jnp.pad(pair_rows, ((0, 0), (1, 1), (0, 0), (0, 0)))
    below_level = from_behind(coef_z[levels - 1 :], "lev", 1)
    vertical = jnp.concatenate(
        [below_level, coef_z, jnp.zeros((1, row_count, cells_y), jnp.float32)], axis=0
    )
    vertical_full = jnp.pad(vertical, ((0, 0), (1, 1), (0, 0)))
    return jnp.stack([pair_full[0], pair_full[1], vertical_full])


def shards(
    state,
    coef_x,
    coef_y,
    coef_z,
    slope,
    compress,
    ground,
    w_in,
    level_table,
    gain_attn,
    w_query,
    w_key,
    w_value,
    w_mix,
    temper,
    gain_head,
    w_tend,
):
    metrics = coefficient_rims(coef_x, slope, coef_z)
    current = state
    for substep in range(SUBSTEPS):
        padded = with_halo(current, (("tile", 2), ("lev", 1)), 1)
        current = acoustic(padded, metrics, coef_y, compress)
    levels = current.shape[1]
    row_count = current.shape[2]
    cells_y = current.shape[3]
    columns = row_count * cells_y
    features = current.astype(jnp.bfloat16).reshape(4, levels, columns)
    ground_marks = jnp.broadcast_to(ground.reshape(1, 1, columns), (1, levels, columns))
    arrived, marks_arrived = (
        lax.all_to_all(features, "lev", split_axis=2, concat_axis=1, tiled=True),
        lax.all_to_all(ground_marks, "lev", split_axis=2, concat_axis=1, tiled=True),
    )
    arrived = embed(arrived, w_in, level_table)
    tendency = physics(
        arrived,
        marks_arrived[0, 0],
        gain_attn,
        w_query,
        w_key,
        w_value,
        w_mix,
        temper,
        gain_head,
        w_tend,
    )
    returned = lax.all_to_all(
        tendency.astype(jnp.bfloat16), "lev", split_axis=1, concat_axis=2, tiled=True
    ).astype(tendency.dtype)
    return current + returned.reshape(4, levels, row_count, cells_y)


def solution(mesh):
    placed = (
        P(None, "lev", "tile", None),
        P("lev", "tile", None),
        P("lev", "tile", None),
        P("lev", "tile", None),
        P("lev", "tile", None),
        P("lev", "tile", None),
        P("tile", None),
        P(),
        P(),
        P(),
        P(),
        P(),
        P(),
        P(),
        P(),
        P(),
        P(),
    )
    return jax.shard_map(
        shards, mesh=mesh, in_specs=placed, out_specs=P(None, "lev", "tile", None), check_vma=False
    )
```

profile of v0, /device:TPU:7, one launch (start us, length us, event | category | flops | bytes accessed | tf_op | source)
XLA Modules:
  0.0 258.8 jit_solution(17369879505766905866)
XLA Ops:
  1.0 4.9 %collective-permute-start = (f32[4,8,1,128]{3,1,2,0:T(8,128)S(1)}, f32[4,8,1,128]{3,1,2,0:T(8,128)S(1)}, u32[]{:S(2)}, u32[]{:S(2)}) collective-permute-start(f32[4,8,1,128]{3,1,2,0:T(8,128)S(1)} %copy.96), channel_id=1, source_target_pairs={{0,4},{4,8},{8,12},{12,16},{16,20},{20,24},{24,28},{28,32},{32,36}... | collective-permute-start | bytes 49160 | tf_op jit(solution)/shard_map/ppermute | solution.py:25
  5.9 7.7 %collective-permute-start.1 = (f32[4,8,1,128]{3,1,2,0:T(8,128)S(1)}, f32[4,8,1,128]{3,1,2,0:T(8,128)S(1)}, u32[]{:S(2)}, u32[]{:S(2)}) collective-permute-start(f32[4,8,1,128]{3,1,2,0:T(8,128)S(1)} %copy.97), channel_id=1, source_target_pairs={{4,0},{8,4},{12,8},{16,12},{20,16},{24,20},{28,24},{32,28},{36,32}... | collective-permute-start | bytes 49160 | tf_op jit(solution)/shard_map/ppermute | solution.py:28
  16.9 3.5 %collective-permute-start.5 = (f32[1,4,128]{2,0,1:T(1,128)S(1)}, f32[1,4,128]{2,0,1:T(1,128)S(1)}, u32[]{:S(2)}, u32[]{:S(2)}) collective-permute-start(f32[1,4,128]{2,0,1:T(1,128)S(1)} %bitcast.189), channel_id=1, source_target_pairs={{0,1},{1,2},{2,3},{4,5},{5,6},{6,7},{8,9},{9,10},{10,11},{12,13},{... | collective-permute-start | bytes 6152 | tf_op jit(solution)/shard_map/ppermute | solution.py:17
  25.2 3.2 %all-to-all-start.1 = ((s32[4,1,1024]{2,1,0:T(1,128)}), s32[4,1,1024]{2,1,0:T(1,128)S(1)}, u32[]{:S(2)}, u32[]{:S(2)}) async-start(s32[4,1,1024]{2,1,0:T(1,128)} %reshape.109), calls=%async_computation.1 | async-start | bytes 32768 | tf_op jit(solution)/shard_map/all_to_all | solution.py:155
  39.6 4.3 %collective-permute-start.6 = (f32[4,8,1,128]{3,1,2,0:T(8,128)S(1)}, f32[4,8,1,128]{3,1,2,0:T(8,128)S(1)}, u32[]{:S(2)}, u32[]{:S(2)}) collective-permute-start(f32[4,8,1,128]{3,1,2,0:T(8,128)S(1)} %get-tuple-element.29), channel_id=1, source_target_pairs={{0,4},{4,8},{8,12},{12,16},{16,20},{20,24},{24,28},{28,32},{32,36}... | collective-permute-start | bytes 49160 | tf_op jit(solution)/shard_map/ppermute | solution.py:25
  43.9 6.2 %collective-permute-start.7 = (f32[4,8,1,128]{3,1,2,0:T(8,128)S(1)}, f32[4,8,1,128]{3,1,2,0:T(8,128)S(1)}, u32[]{:S(2)}, u32[]{:S(2)}) collective-permute-start(f32[4,8,1,128]{3,1,2,0:T(8,128)S(1)} %get-tuple-element.30), channel_id=1, source_target_pairs={{4,0},{8,4},{12,8},{16,12},{20,16},{24,20},{28,24},{32,28},{36,32}... | collective-permute-start | bytes 49160 | tf_op jit(solution)/shard_map/ppermute | solution.py:28
  63.3 8.5 %collective-permute-start.11 = (f32[4,8,1,128]{3,1,2,0:T(8,128)S(1)}, f32[4,8,1,128]{3,1,2,0:T(8,128)S(1)}, u32[]{:S(2)}, u32[]{:S(2)}) collective-permute-start(f32[4,8,1,128]{3,1,2,0:T(8,128)S(1)} %get-tuple-element.28), channel_id=1, source_target_pairs={{4,0},{8,4},{12,8},{16,12},{20,16},{24,20},{28,24},{32,28},{36,32}... | collective-permute-start | bytes 49160 | tf_op jit(solution)/shard_map/ppermute | solution.py:28
  84.1 3.4 %all-to-all-start = ((bf16[4,2,2048]{2,1,0:T(2,128)(2,1)}), bf16[4,2,2048]{2,1,0:T(2,128)(2,1)S(1)}, u32[]{:S(2)}, u32[]{:S(2)}) async-start(bf16[4,2,2048]{2,1,0:T(2,128)(2,1)} %reshape.107), calls=%async_computation | async-start | bytes 65536 | tf_op jit(solution)/shard_map/all_to_all | solution.py:154
  93.8 4.6 %convolution_bitcast_fusion = f32[512,32,128]{0,2,1:T(8,128)} fusion(bf16[512,32,128]{0,2,1:T(8,128)(2,1)S(1)} %get-tuple-element.44, f32[512]{0:T(512)S(1)} %copy-done.12, f32[32,128]{1,0:T(8,128)S(1)} %add_rsqrt_fusion.3, bf16[512,512]{1,0:T(8,128)(2,1)S(1)} %copy-done.7), kind=kOutput, calls=%fused_computation.27 | convolution fusion | flops 2155872256 | bytes 13125632 | tf_op jit(solution)/shard_map/dlc,de->elc/dot_general | solution.py:62
  98.4 10.3 %copy.73 = f32[512,32,128]{2,1,0:T(8,128)} copy(f32[512,32,128]{0,2,1:T(8,128)} %convolution_bitcast_fusion) | data formatting | bytes 16777216 | tf_op jit(solution)/shard_map/dlc,de->elc/dot_general | solution.py:62
  108.7 4.7 %multiply_reduce_fusion.1 = f32[8,32,128]{2,1,0:T(8,128)S(1)} fusion(f32[512,32,128]{2,1,0:T(8,128)} %copy.73), kind=kLoop, calls=%fused_computation.21 | loop fusion | flops 4161536 | bytes 8519680 | tf_op jit(solution)/shard_map/reduce_sum | solution.py:66
  117.5 15.7 %copy.75 = bf16[8,64,32,128]{1,2,3,0:T(8,128)(2,1)} copy(bf16[8,64,32,128]{3,2,1,0:T(8,128)(2,1)} %multiply_convert_fusion.1) | data formatting | bytes 8388608 | tf_op jit(solution)/shard_map/convert_element_type | solution.py:88
  133.2 7.8 %convolution_bitcast_fusion.1 = f32[512,32,128]{0,2,1:T(8,128)} fusion(bf16[512,32,128]{0,2,1:T(8,128)(2,1)} %copy-done.3, f32[512]{0:T(512)S(1)} %copy-done.12, f32[32,128]{1,0:T(8,128)S(1)} %add_rsqrt_fusion.3, bf16[512,512]{1,0:T(8,128)(2,1)S(1)} %copy-done.8), kind=kOutput, calls=%fused_computation.28 | convolution fusion | flops 2155872256 | bytes 13125632 | tf_op jit(solution)/shard_map/dlc,de->elc/dot_general | solution.py:62
  141.1 10.3 %copy.72 = f32[512,32,128]{2,1,0:T(8,128)} copy(f32[512,32,128]{0,2,1:T(8,128)} %convolution_bitcast_fusion.1) | data formatting | bytes 16777216 | tf_op jit(solution)/shard_map/dlc,de->elc/dot_general | solution.py:62
  151.3 4.7 %multiply_reduce_fusion.2 = f32[8,32,128]{2,1,0:T(8,128)S(1)} fusion(f32[512,32,128]{2,1,0:T(8,128)} %copy.72), kind=kLoop, calls=%fused_computation.23 | loop fusion | flops 4161536 | bytes 8519680 | tf_op jit(solution)/shard_map/reduce_sum | solution.py:66
  160.3 15.6 %copy.74 = bf16[8,64,32,128]{1,2,3,0:T(8,128)(2,1)} copy(bf16[8,64,32,128]{3,2,1,0:T(8,128)(2,1)} %multiply_convert_fusion.2) | data formatting | bytes 8388608 | tf_op jit(solution)/shard_map/convert_element_type | solution.py:89
  175.9 6.7 %convert_bitcast_fusion.1 = bf16[512,32,128]{0,2,1:T(8,128)(2,1)} fusion(bf16[512,32,128]{0,2,1:T(8,128)(2,1)} %copy-done.3, f32[512]{0:T(512)S(1)} %copy-done.12, f32[32,128]{1,0:T(8,128)S(1)} %add_rsqrt_fusion.3, bf16[512,512]{1,0:T(8,128)(2,1)S(1)} %copy-done.9), kind=kOutput, calls=%fused_computation.25 | convolution fusion | flops 2157969408 | bytes 8931328 | tf_op jit(solution)/shard_map/dlc,de->elc/dot_general | solution.py:62
  182.6 7.9 %copy.70 = bf16[512,32,128]{2,1,0:T(8,128)(2,1)} copy(bf16[512,32,128]{0,2,1:T(8,128)(2,1)} %convert_bitcast_fusion.1) | data formatting | bytes 8388608 | tf_op jit(solution)/shard_map/convert_element_type | solution.py:90
  190.5 15.6 %copy.76 = bf16[8,64,32,128]{1,2,3,0:T(8,128)(2,1)} copy(bf16[8,64,32,128]{3,2,1,0:T(8,128)(2,1)} %bitcast.167) | data formatting | bytes 8388608 | tf_op jit(solution)/shard_map/convert_element_type | solution.py:90
  206.1 14.2 %fusion.69 = (f32[8,32,128]{1,2,0:T(8,128)S(1)}, f32[8,32,32,128]{1,2,3,0:T(8,128)}) fusion(f32[8]{0:T(128)S(1)} %broadcast_multiply_fusion, pred[32,128]{0,1:T(8,128)(4,1)S(1)} %iota_compare_fusion, bf16[8,64,32,128]{1,2,3,0:T(8,128)(2,1)} %copy.74, bf16[8,64,32,128]{1,2,3,0:T(8,128)(2,1)} %copy.75), kind=kOutput, calls=%fused_computation.174 | convolution fusion | flops 138412064 | bytes 12718112 | tf_op jit(solution)/shard_map/sub | solution.py:98
  220.3 13.3 %convert_bitcast_fusion = bf16[8,64,32,128]{1,2,3,0:T(8,128)(2,1)} fusion(bf16[8,64,32,128]{1,2,3,0:T(8,128)(2,1)} %copy.76, f32[8,32,32,128]{1,2,3,0:T(8,128)} %get-tuple-element.46, f32[8,32,128]{1,2,0:T(8,128)S(1)} %get-tuple-element.45), kind=kOutput, calls=%fused_computation.16 | convolution fusion | flops 138412032 | bytes 12713984 | tf_op jit(solution)/shard_map/hlmc,hjmc->hjlc/dot_general | solution.py:62
  233.6 9.8 %copy.85 = bf16[8,64,32,128]{3,1,0,2:T(8,128)(2,1)} copy(bf16[8,64,32,128]{1,2,3,0:T(8,128)(2,1)} %convert_bitcast_fusion) | data formatting | bytes 8388608 | tf_op jit(solution)/shard_map/reshape | solution.py:101
  243.5 6.6 %multiply_reduce_fusion = (f32[32,128]{1,0:T(8,128)S(1)}, f32[32,128,512]{2,1,0:T(8,128)S(1)}) fusion(bf16[512,32,128]{0,2,1:T(8,128)(2,1)} %copy-done.3, bf16[512,32,128]{2,0,1:T(8,128)(2,1)} %bitcast.166, bf16[512,512]{1,0:T(8,128)(2,1)S(1)} %copy-done), kind=kOutput, calls=%fused_computation.15 | convolution fusion | flops 2155868160 | bytes 17317888 | tf_op jit(solution)/shard_map/dlc,de->elc/dot_general | solution.py:62
  251.8 6.3 %all_to_all.45 = bf16[4,32,128]{2,0,1:T(4,128)(2,1)S(1)} all-to-all(bf16[4,32,128]{2,0,1:T(4,128)(2,1)S(1)} %fusion.16), channel_id=1, replica_groups=mesh['tile'=64,'lev'=4] {'lev'}, dimensions={1} | all-to-all | bytes 65536 | tf_op jit(solution)/shard_map/all_to_all | solution.py:170
  (127 shorter events, 62.5 us)
Async XLA Ops:
  0.0 243.4 %copy-start = (bf16[512,512]{1,0:T(8,128)(2,1)S(1)}, bf16[512,512]{1,0:T(8,128)(2,1)}, u32[]{:S(2)}) copy-start(bf16[512,512]{1,0:T(8,128)(2,1)} %param.30) | copy-start | bytes 1572868
  0.0 90.1 %copy-start.10 = (f32[32,512]{1,0:T(8,128)S(1)}, f32[32,512]{1,0:T(8,128)}, u32[]{:S(2)}) copy-start(f32[32,512]{1,0:T(8,128)} %param.25) | copy-start | bytes 196612
  0.0 90.1 %copy-start.11 = (bf16[4,512]{1,0:T(4,128)(2,1)S(1)}, bf16[4,512]{1,0:T(4,128)(2,1)}, u32[]{:S(2)}) copy-start(bf16[4,512]{1,0:T(4,128)(2,1)} %param.24) | copy-start | bytes 12292
  1.0 28.4 %collective-permute-start = (f32[4,8,1,128]{3,1,2,0:T(8,128)S(1)}, f32[4,8,1,128]{3,1,2,0:T(8,128)S(1)}, u32[]{:S(2)}, u32[]{:S(2)}) collective-permute-start(f32[4,8,1,128]{3,1,2,0:T(8,128)S(1)} %copy.96), channel_id=1, source_target_pairs={{0,4},{4,8},{8,12},{12,16},{16,20},{20,24},{24,28},{28,32},{32,36}... | collective-permute-start | bytes 49160 | tf_op jit(solution)/shard_map/ppermute | solution.py:25
  5.9 24.3 %collective-permute-start.1 = (f32[4,8,1,128]{3,1,2,0:T(8,128)S(1)}, f32[4,8,1,128]{3,1,2,0:T(8,128)S(1)}, u32[]{:S(2)}, u32[]{:S(2)}) collective-permute-start(f32[4,8,1,128]{3,1,2,0:T(8,128)S(1)} %copy.97), channel_id=1, source_target_pairs={{4,0},{8,4},{12,8},{16,12},{20,16},{24,20},{28,24},{32,28},{36,32}... | collective-permute-start | bytes 49160 | tf_op jit(solution)/shard_map/ppermute | solution.py:28
  14.3 14.9 %collective-permute-start.4 = (f32[2,8,1,128]{3,1,2,0:T(8,128)S(1)}, f32[2,8,1,128]{3,1,2,0:T(8,128)S(1)}, u32[]{:S(2)}, u32[]{:S(2)}) collective-permute-start(f32[2,8,1,128]{3,1,2,0:T(8,128)S(1)} %pad_maximum_fusion.27), channel_id=1, source_target_pairs={{0,4},{4,8},{8,12},{12,16},{16,20},{20,24},{24,28},{28,32},{32,36}... | collective-permute-start | bytes 24584 | tf_op jit(solution)/shard_map/ppermute | solution.py:17
  16.9 21.8 %collective-permute-start.5 = (f32[1,4,128]{2,0,1:T(1,128)S(1)}, f32[1,4,128]{2,0,1:T(1,128)S(1)}, u32[]{:S(2)}, u32[]{:S(2)}) collective-permute-start(f32[1,4,128]{2,0,1:T(1,128)S(1)} %bitcast.189), channel_id=1, source_target_pairs={{0,1},{1,2},{2,3},{4,5},{5,6},{6,7},{8,9},{9,10},{10,11},{12,13},{... | collective-permute-start | bytes 6152 | tf_op jit(solution)/shard_map/ppermute | solution.py:17
  20.4 73.4 %copy-start.7 = (bf16[512,512]{1,0:T(8,128)(2,1)S(1)}, bf16[512,512]{1,0:T(8,128)(2,1)}, u32[]{:S(2)}) copy-start(bf16[512,512]{1,0:T(8,128)(2,1)} %param.27) | copy-start | bytes 1572868
  20.4 73.4 %copy-start.12 = (f32[512]{0:T(512)S(1)}, f32[512]{0:T(512)}, u32[]{:S(2)}) copy-start(f32[512]{0:T(512)} %param.26) | copy-start | bytes 6148
  25.2 25.6 %all-to-all-start.1 = ((s32[4,1,1024]{2,1,0:T(1,128)}), s32[4,1,1024]{2,1,0:T(1,128)S(1)}, u32[]{:S(2)}, u32[]{:S(2)}) async-start(s32[4,1,1024]{2,1,0:T(1,128)} %reshape.109), calls=%async_computation.1 | async-start | bytes 32768 | tf_op jit(solution)/shard_map/all_to_all | solution.py:155
  30.3 4.4 %collective-permute-start.2 = (f32[4,1,6,128]{3,1,2,0:T(1,128)S(1)}, f32[4,1,6,128]{3,1,2,0:T(1,128)S(1)}, u32[]{:S(2)}, u32[]{:S(2)}) collective-permute-start(f32[4,1,6,128]{3,1,2,0:T(1,128)S(1)} %get-tuple-element.25), channel_id=1, source_target_pairs={{0,1},{1,2},{2,3},{4,5},{5,6},{6,7},{8,9},{9,10},{10,11},{12,13},{... | collective-permute-start | bytes 36872 | tf_op jit(solution)/shard_map/ppermute | solution.py:25
  32.7 5.0 %collective-permute-start.3 = (f32[4,1,6,128]{3,1,2,0:T(1,128)S(1)}, f32[4,1,6,128]{3,1,2,0:T(1,128)S(1)}, u32[]{:S(2)}, u32[]{:S(2)}) collective-permute-start(f32[4,1,6,128]{3,1,2,0:T(1,128)S(1)} %get-tuple-element.26), channel_id=1, source_target_pairs={{1,0},{2,1},{3,2},{5,4},{6,5},{7,6},{9,8},{10,9},{11,10},{13,12},{... | collective-permute-start | bytes 36872 | tf_op jit(solution)/shard_map/ppermute | solution.py:28
  39.6 12.5 %collective-permute-start.6 = (f32[4,8,1,128]{3,1,2,0:T(8,128)S(1)}, f32[4,8,1,128]{3,1,2,0:T(8,128)S(1)}, u32[]{:S(2)}, u32[]{:S(2)}) collective-permute-start(f32[4,8,1,128]{3,1,2,0:T(8,128)S(1)} %get-tuple-element.29), channel_id=1, source_target_pairs={{0,4},{4,8},{8,12},{12,16},{16,20},{20,24},{24,28},{28,32},{32,36}... | collective-permute-start | bytes 49160 | tf_op jit(solution)/shard_map/ppermute | solution.py:25
  43.9 8.2 %collective-permute-start.7 = (f32[4,8,1,128]{3,1,2,0:T(8,128)S(1)}, f32[4,8,1,128]{3,1,2,0:T(8,128)S(1)}, u32[]{:S(2)}, u32[]{:S(2)}) collective-permute-start(f32[4,8,1,128]{3,1,2,0:T(8,128)S(1)} %get-tuple-element.30), channel_id=1, source_target_pairs={{4,0},{8,4},{12,8},{16,12},{20,16},{24,20},{28,24},{32,28},{36,32}... | collective-permute-start | bytes 49160 | tf_op jit(solution)/shard_map/ppermute | solution.py:28
  52.1 4.4 %collective-permute-start.8 = (f32[4,1,6,128]{3,1,2,0:T(1,128)S(1)}, f32[4,1,6,128]{3,1,2,0:T(1,128)S(1)}, u32[]{:S(2)}, u32[]{:S(2)}) collective-permute-start(f32[4,1,6,128]{3,1,2,0:T(1,128)S(1)} %get-tuple-element.23), channel_id=1, source_target_pairs={{0,1},{1,2},{2,3},{4,5},{5,6},{6,7},{8,9},{9,10},{10,11},{12,13},{... | collective-permute-start | bytes 36872 | tf_op jit(solution)/shard_map/ppermute | solution.py:25
  54.5 5.0 %collective-permute-start.9 = (f32[4,1,6,128]{3,1,2,0:T(1,128)S(1)}, f32[4,1,6,128]{3,1,2,0:T(1,128)S(1)}, u32[]{:S(2)}, u32[]{:S(2)}) collective-permute-start(f32[4,1,6,128]{3,1,2,0:T(1,128)S(1)} %get-tuple-element.24), channel_id=1, source_target_pairs={{1,0},{2,1},{3,2},{5,4},{6,5},{7,6},{9,8},{10,9},{11,10},{13,12},{... | collective-permute-start | bytes 36872 | tf_op jit(solution)/shard_map/ppermute | solution.py:28
  61.4 10.4 %collective-permute-start.10 = (f32[4,8,1,128]{3,1,2,0:T(8,128)S(1)}, f32[4,8,1,128]{3,1,2,0:T(8,128)S(1)}, u32[]{:S(2)}, u32[]{:S(2)}) collective-permute-start(f32[4,8,1,128]{3,1,2,0:T(8,128)S(1)} %get-tuple-element.27), channel_id=1, source_target_pairs={{0,4},{4,8},{8,12},{12,16},{16,20},{20,24},{24,28},{28,32},{32,36}... | collective-permute-start | bytes 49160 | tf_op jit(solution)/shard_map/ppermute | solution.py:25
  63.3 9.4 %collective-permute-start.11 = (f32[4,8,1,128]{3,1,2,0:T(8,128)S(1)}, f32[4,8,1,128]{3,1,2,0:T(8,128)S(1)}, u32[]{:S(2)}, u32[]{:S(2)}) collective-permute-start(f32[4,8,1,128]{3,1,2,0:T(8,128)S(1)} %get-tuple-element.28), channel_id=1, source_target_pairs={{4,0},{8,4},{12,8},{16,12},{20,16},{24,20},{28,24},{32,28},{36,32}... | collective-permute-start | bytes 49160 | tf_op jit(solution)/shard_map/ppermute | solution.py:28
  72.7 5.0 %collective-permute-start.12 = (f32[4,1,6,128]{3,1,2,0:T(1,128)S(1)}, f32[4,1,6,128]{3,1,2,0:T(1,128)S(1)}, u32[]{:S(2)}, u32[]{:S(2)}) collective-permute-start(f32[4,1,6,128]{3,1,2,0:T(1,128)S(1)} %get-tuple-element.21), channel_id=1, source_target_pairs={{0,1},{1,2},{2,3},{4,5},{5,6},{6,7},{8,9},{9,10},{10,11},{12,13},{... | collective-permute-start | bytes 36872 | tf_op jit(solution)/shard_map/ppermute | solution.py:25
  75.8 5.0 %collective-permute-start.13 = (f32[4,1,6,128]{3,1,2,0:T(1,128)S(1)}, f32[4,1,6,128]{3,1,2,0:T(1,128)S(1)}, u32[]{:S(2)}, u32[]{:S(2)}) collective-permute-start(f32[4,1,6,128]{3,1,2,0:T(1,128)S(1)} %get-tuple-element.22), channel_id=1, source_target_pairs={{1,0},{2,1},{3,2},{5,4},{6,5},{7,6},{9,8},{10,9},{11,10},{13,12},{... | collective-permute-start | bytes 36872 | tf_op jit(solution)/shard_map/ppermute | solution.py:28
  84.1 5.0 %all-to-all-start = ((bf16[4,2,2048]{2,1,0:T(2,128)(2,1)}), bf16[4,2,2048]{2,1,0:T(2,128)(2,1)S(1)}, u32[]{:S(2)}, u32[]{:S(2)}) async-start(bf16[4,2,2048]{2,1,0:T(2,128)(2,1)} %reshape.107), calls=%async_computation | async-start | bytes 65536 | tf_op jit(solution)/shard_map/all_to_all | solution.py:154
  117.5 15.7 %copy-start.8 = (bf16[512,512]{1,0:T(8,128)(2,1)S(1)}, bf16[512,512]{1,0:T(8,128)(2,1)}, u32[]{:S(2)}) copy-start(bf16[512,512]{1,0:T(8,128)(2,1)} %param.28) | copy-start | bytes 1572868
  160.3 15.6 %copy-start.9 = (bf16[512,512]{1,0:T(8,128)(2,1)S(1)}, bf16[512,512]{1,0:T(8,128)(2,1)}, u32[]{:S(2)}) copy-start(bf16[512,512]{1,0:T(8,128)(2,1)} %param.29) | copy-start | bytes 1572868
  243.4 6.6 %copy-start.6 = (f32[512]{0:T(512)S(1)}, f32[512]{0:T(512)}, u32[]{:S(2)}) copy-start(f32[512]{0:T(512)} %param.32) | copy-start | bytes 6148
  (5 other events, 26.7 us)
where the time goes:
time: 261 us; the launch traced here: 259 us
  local copies, waits for them, and re-layouts  101 us (39%)
  starting transfers between devices  59.2 us (23%)
  matrix products  56.8 us (22%)
  other arithmetic  23.7 us (9%)
  waiting for transfers between devices  11.5 us (4%)
  blocking collectives  6.32 us (2%)
    dot_general x7, matrix products, multiply(): jnp.einsum(pattern, first_op, second_op, preferred_element_type=jnp.float32)  42.5 us
    ppermute x6, starting transfers between devices, with_halo(): lax.ppermute(lax.slice_in_dim(block, 0, width, axis=dim), axis, backward)  28.1 us
    convert_element_type x2, local copies, waits for them, and re-layouts, physics(): value_heads = heads_of(w_value).astype(jnp.bfloat16)  23.5 us
    dot_general x2, local copies, waits for them, and re-layouts, multiply(): jnp.einsum(pattern, first_op, second_op, preferred_element_type=jnp.float32)  20.6 us
    ppermute x6, starting transfers between devices, with_halo(): lax.ppermute(lax.slice_in_dim(block, block.shape[dim] - width, None, axis...  19 us
    convert_element_type x1, local copies, waits for them, and re-layouts, physics(): query_heads = rms_scale(heads_of(w_query), 1).astype(jnp.bfloat16)  15.7 us
    convert_element_type x1, local copies, waits for them, and re-layouts, physics(): key_heads = rms_scale(heads_of(w_key), 1).astype(jnp.bfloat16)  15.6 us
    sub x1, matrix products, physics(): weights = jnp.exp(scores - peak)  14.2 us
  transfers between devices with their start and end apart: 16, of which 5 were waited for; matrix products, arithmetic and copies ran while one was open for 5% of the time, Pallas kernels for 0%

commit v1 on v0

v1 whole, which is shorter than its diff:
```python
import math

import jax
import jax.numpy as jnp
from jax import lax
from jax.experimental import pallas as pl
from jax.experimental.pallas import tpu as pltpu
from jax.sharding import PartitionSpec as P

EPS = 1e-6
F32, BF16 = jnp.float32, jnp.bfloat16
LOG2E = math.log2(math.e)
HEADS, WIDTH, LEVELS, CELLS = 8, 512, 32, 128
HS = WIDTH // HEADS
X = 40


def dot(a, b):
    return jnp.dot(a, b, preferred_element_type=F32)


def dot_t(a, b):
    return lax.dot_general(a, b, (((1,), (1,)), ((), ())), precision=lax.Precision.HIGHEST, preferred_element_type=F32)


def split3(a):
    hi = a.astype(BF16).astype(F32)
    mid = (a - hi).astype(BF16).astype(F32)
    return hi, mid, a - hi - mid


def spread(a):
    hi, mid, lo = split3(a)
    return (hi + pltpu.roll(mid, X, 1) + pltpu.roll(lo, 2 * X, 1)).astype(BF16)


def prepare_maps(w_in, table, gain_attn, wq, wk, wv, wm, gain_head, w_tend, temper, lk, ls, lf, tcol):
    emb = jnp.concatenate([w_in[...].astype(F32), jnp.zeros((4, WIDTH), F32), table[...]], axis=0)
    xg3 = jnp.concatenate(split3(emb * gain_attn[...]), axis=0).astype(BF16)

    def through(w):
        a = dot(xg3, w[...])
        return a[:X] + a[X : 2 * X] + a[2 * X :]

    aq, ak, av = through(wq), through(wk), through(wv)
    pad = jnp.zeros((128 - X, WIDTH), F32)
    aq_p = jnp.concatenate([aq, pad], axis=0)
    ak_p = jnp.concatenate([ak, pad], axis=0)
    head = lax.broadcasted_iota(jnp.int32, (X, WIDTH), 1) // HS

    def by_head(a):
        return jnp.concatenate([jnp.where(head == h, a, 0.0) for h in range(HEADS)], axis=0)

    kb = by_head(ak)
    qb = by_head(aq)
    s_map = dot_t(kb, aq_p)
    kk = dot_t(kb, ak_p)
    qq = dot_t(qb, aq_p)
    ee = dot_t(emb, jnp.concatenate([emb, pad], axis=0))
    lane = lax.broadcasted_iota(jnp.int32, (1, 128), 1)
    twice = jnp.where(lane < 8, 1.0, 2.0)
    r40 = lax.broadcasted_iota(jnp.int32, (X, 128), 0)
    l40 = lax.broadcasted_iota(jnp.int32, (X, 128), 1)
    diag = (r40 == l40) & (r40 >= 8)

    def norm_rows(g):
        return [g[i : i + 1] * twice for i in range(4)] + [jnp.sum(jnp.where(diag, g, 0.0), axis=0, keepdims=True)]

    def norm_map(gram):
        per = [norm_rows(gram[X * h : X * h + X]) for h in range(HEADS)]
        return jnp.concatenate([per[h][i] for i in range(5) for h in range(HEADS)], axis=0)

    e_rows = norm_rows(ee) + [jnp.zeros((3, 128), F32)]
    lk[...] = spread(jnp.concatenate([norm_map(kk)] + e_rows, axis=0))
    ls[0:320] = spread(s_map)
    ls[320:360] = spread(norm_map(qq))
    ls[360:368] = jnp.zeros((8, 128), BF16)

    vh, vm, _ = split3(by_head(av))
    c = dot(vh.astype(BF16), wm[...]) + dot(vm.astype(BF16), wm[...])
    eh, em, el = split3(emb)
    rows = [c[X * h + 8 : X * h + X] for h in range(HEADS)]
    rows += [jnp.broadcast_to(c[X * h + i : X * h + i + 1], (8, WIDTH)) for h in range(HEADS) for i in range(4)]
    rows += [eh, em, el, jnp.zeros((8, WIDTH), F32)]
    lft = jnp.concatenate(rows, axis=0)
    wt = jnp.concatenate([w_tend[...].astype(F32), jnp.zeros((12, WIDTH), F32)], axis=0) * gain_head[...]
    t = dot_t(wt, lft)
    th = t[:8].astype(BF16).astype(F32)
    lf[0:512] = lft.T.astype(BF16)
    lf[512:528] = jnp.concatenate([th, t[:8] - th], axis=0).astype(BF16)
    row8 = lax.broadcasted_iota(jnp.int32, (8, 128), 0)
    tc = jnp.zeros((8, 128), F32)
    for h in range(HEADS):
        tc = jnp.where(row8 == h, temper[h] * (LOG2E / math.sqrt(HS)), tc)
    tcol[...] = tc


def token_rows(fl, l):
    lev = lax.broadcasted_iota(jnp.int32, (LEVELS, CELLS), 0) == l
    one = jnp.concatenate([fl[l], lev.astype(F32)], axis=0)
    return jnp.concatenate([one, one, one, jnp.zeros((8, CELLS), F32)], axis=0).astype(BF16)


def norms_at(out, f, base, epsq, scale):
    n = out[base + 32 : base + 40]
    for i in range(4):
        n = n + f[i : i + 1] * out[base + 8 * i : base + 8 * i + 8]
    return lax.rsqrt(jnp.maximum(n, 0.0) * (1.0 / HS) + epsq) * scale


def key_pass(l, fl, lk, rk, rs, eq):
    out = dot(lk[...], token_rows(fl, l))
    f = fl[l]
    n = out[44:45]
    for i in range(4):
        n = n + f[i : i + 1] * out[40 + i : 41 + i]
    ms = jnp.maximum(n, 0.0) * (1.0 / WIDTH) + EPS
    rs[pl.ds(l, 1), :] = lax.rsqrt(ms)
    eq[pl.ds(l, 1), :] = EPS * ms
    rk[:, l, :] = norms_at(out, f, 0, EPS * ms, 1.0)


def query_pass(l0, fl, fm, bias, ls, lf, tcol, rk, rs, eq, ot):
    x = jnp.concatenate([token_rows(fl, l0), token_rows(fl, l0 + 1)], axis=1)
    out = dot(ls[...], x)
    parts = []
    for a in range(2):
        o = out[:, 128 * a : 128 * a + 128]
        rq = norms_at(o, fl[l0 + a], 320, eq[pl.ds(l0 + a, 1), :], tcol[...])
        probs, sums = [], []
        for h in range(HEADS):
            s = o[X * h + 8 : X * h + X]
            for i in range(4):
                s = s + fm[i] * o[X * h + i : X * h + i + 1]
            s = s * rk[h] * rq[h : h + 1] + bias[...]
            p = jnp.exp2(s - jnp.max(s, axis=0, keepdims=True))
            p = p * (1.0 / jnp.sum(p, axis=0, keepdims=True)) * rs[...]
            probs.append(p)
            for i in range(4):
                z = p * fm[i]
                sums.append(z[0:8] + z[8:16] + z[16:24] + z[24:32])
        parts.append(jnp.concatenate(probs + sums, axis=0).astype(BF16))
    rhs = jnp.concatenate([jnp.concatenate(parts, axis=1), x], axis=0)
    fin = dot(lf[...], rhs)
    stream = fin[:512]
    ms = jnp.mean(stream * stream, axis=0, keepdims=True)
    tend = (fin[512:520] + fin[520:528]) * lax.rsqrt(ms + EPS)
    ot[l0] = tend[:, :128]
    ot[l0 + 1] = tend[:, 128:]


ROWS = 4
KL = 8
MESH = pl.DeviceIdType.MESH


def level_above(a, row):
    k = lax.broadcasted_iota(jnp.int32, (KL, CELLS), 0)
    return jnp.where(k == KL - 1, row, pltpu.roll(a, KL - 1, 0))


def level_below(a, row):
    k = lax.broadcasted_iota(jnp.int32, (KL, CELLS), 0)
    return jnp.where(k == 0, row, pltpu.roll(a, 1, 0))


def substep(p, p_lo, p_hi, u, v, w, w_lo, cx, sl, cy, cz, cz_lo, cp):
    up = [level_above(p[i], p_hi[i]) for i in range(ROWS + 1)]
    down = [level_below(p[i], p_lo[i]) for i in range(ROWS + 1)]
    u = [u[i] - cx[i] * (p[i + 1] - p[i]) - 0.5 * sl[i] * (up[i] - down[i]) for i in range(ROWS + 1)]
    new_p, new_v, new_w, new_w_lo = [], [], [], []
    for x in range(ROWS):
        c = p[x + 1]
        wx = w[x] - cz[x] * (up[x + 1] - c)
        wl = w_lo[x] - cz_lo[x] * (c[0:1] - p_lo[x + 1])
        vx = v[x] - cy[x] * (pltpu.roll(c, CELLS - 1, 1) - c)
        div = (u[x + 1] - u[x]) + (vx - pltpu.roll(vx, 1, 1)) + (wx - level_below(wx, wl))
        new_p.append(c - cp[x] * div)
        new_v.append(vx)
        new_w.append(wx)
        new_w_lo.append(wl)
    return new_p, u, new_v, new_w, new_w_lo


def whole(tiles, levs, state, coef_x, coef_y, coef_z, slope, compress, ground, temper,
          w_in, table, gain_attn, gain_head, w_tend, wq_hbm, wk_hbm, wv_hbm, wm_hbm, out,
          fl, ot, lk, ls, lf, tcol, rk, rs, eq, bias, fm,
          wq, wk, wv, wm, w_sem,
          up0_s, up0_r, up_s, up_r, dn_s, dn_r, kup0_s, kup0_r, kup_s, kup_r, kdn_s, kdn_r,
          cu_s, cu_r, cd_s, cd_r, halo_ss, halo_rs,
          feat_s, feat_r, feat_ss, feat_rs, tend_s, tend_r, tend_ss, tend_rs, cur):
    tile, lev = lax.axis_index("tile"), lax.axis_index("lev")
    east, west = lax.rem(tile + 1, tiles), lax.rem(tile + tiles - 1, tiles)
    above, below = lax.rem(lev + 1, levs), lax.rem(lev + levs - 1, levs)

    weights = [
        pltpu.make_async_copy(src, dst, w_sem.at[n])
        for n, (src, dst) in enumerate(((wq_hbm, wq), (wk_hbm, wk), (wv_hbm, wv), (wm_hbm, wm)))
    ]
    for copy in weights:
        copy.start()

    barrier = pltpu.get_barrier_semaphore()
    partners = [(east, lev), (west, lev), (east, above), (east, below), (west, above), (west, below)]
    partners += [(tile, lax.rem(lev + d, levs)) for d in range(1, levs)]
    for partner in partners:
        pl.semaphore_signal(barrier, inc=1, device_id=partner, device_id_type=MESH)

    def slab(ref, x, f=0):
        return ref[pl.ds(f * KL * ROWS + x, KL, stride=ROWS), :]

    def level(ref, k, f=0):
        return ref[(f * KL + k) * ROWS : (f * KL + k + 1) * ROWS, :]

    top = KL - 1
    up0_s[...] = jnp.concatenate(
        [slab(state, 3, 0), slab(state, 3, 1), slab(coef_x, 3), slab(slope, 3)], axis=0
    )
    kup0_s[...] = jnp.concatenate([level(state, top, 0), level(state, top, 3), level(coef_z, top)], axis=0)

    def halo_copies(n):
        routes = (
            (up0_s if n == 0 else up_s.at[n - 1], up0_r if n == 0 else up_r.at[n - 1], (east, lev)),
            (dn_s.at[n], dn_r.at[n], (west, lev)),
            (kup0_s if n == 0 else kup_s.at[n - 1], kup0_r if n == 0 else kup_r.at[n - 1], (tile, above)),
            (kdn_s.at[n], kdn_r.at[n], (tile, below)),
            (cu_s.at[n], cu_r.at[n], (east, above)),
            (cd_s.at[n], cd_r.at[n], (east, below)),
        )
        return [
            pltpu.make_async_remote_copy(
                src_ref=src, dst_ref=dst, send_sem=halo_ss.at[n, i], recv_sem=halo_rs.at[n, i],
                device_id=where, device_id_type=MESH,
            )
            for i, (src, dst, where) in enumerate(routes)
        ]

    def send_pressure(n, p):
        if n > 0:
            up_s[n - 1] = p[3]
            kup_s[n - 1] = jnp.concatenate([a[top:] for a in p], axis=0)
        dn_s[n] = p[0]
        kdn_s[n] = jnp.concatenate([a[0:1] for a in p], axis=0)
        cu_s[n] = p[3][top:]
        cd_s[n] = p[3][0:1]

    p = [slab(state, x, 0) for x in range(ROWS)]
    send_pressure(0, p)
    pl.semaphore_wait(barrier, len(partners))
    copies = halo_copies(0)
    for copy in copies:
        copy.start()

    in_west = (tile > 0).astype(F32)
    in_east = (tile < tiles - 1).astype(F32)
    in_below = (lev > 0).astype(F32)
    in_above = (lev < levs - 1).astype(F32)

    for copy in weights:
        copy.wait()
    m_level = lax.broadcasted_iota(jnp.int32, (LEVELS, CELLS), 0)
    bias[...] = jnp.where(m_level >= ground[pl.ds(lev, 1), :], 0.0, -1e30)
    prepare_maps(w_in, table, gain_attn, wq, wk, wv, wm, gain_head, w_tend, temper, lk, ls, lf, tcol)

    u = [None] + [slab(state, x, 1) for x in range(ROWS)]
    v = [slab(state, x, 2) for x in range(ROWS)]
    w = [slab(state, x, 3) for x in range(ROWS)]
    cx = [None] + [slab(coef_x, x) for x in range(ROWS)]
    sl = [None] + [slab(slope, x) for x in range(ROWS)]
    cy = [slab(coef_y, x) for x in range(ROWS)]
    cz = [slab(coef_z, x) for x in range(ROWS)]
    cp = [slab(compress, x) for x in range(ROWS)]
    w_lo = cz_lo = None
    for n in range(3):
        for copy in copies:
            copy.wait()
        if n == 0:
            west_p = up0_r[0:KL] * in_west
            u[0] = up0_r[KL : 2 * KL] * in_west
            cx[0] = up0_r[2 * KL : 3 * KL] * in_west
            sl[0] = up0_r[3 * KL : 4 * KL] * in_west
            low = kup0_r[...] * in_below
            p_lo = [low[x : x + 1] for x in range(ROWS)]
            w_lo = [low[ROWS + x : ROWS + x + 1] for x in range(ROWS)]
            cz_lo = [low[2 * ROWS + x : 2 * ROWS + x + 1] for x in range(ROWS)]
        else:
            west_p = up_r[n - 1] * in_west
            low = kup_r[n - 1] * in_below
            p_lo = [low[x : x + 1] for x in range(ROWS)]
        high = kdn_r[n] * in_above
        p_lo = [cu_r[n] * (in_west * in_below)] + p_lo
        p_hi = [cd_r[n] * (in_west * in_above)] + [high[x : x + 1] for x in range(ROWS)]
        east_p = dn_r[n] * in_east
        p, u, v, w, w_lo = substep([west_p] + p + [east_p], p_lo, p_hi, u, v, w, w_lo, cx, sl, cy, cz, cz_lo, cp)
        if n < 2:
            send_pressure(n + 1, p)
            copies = halo_copies(n + 1)
            for copy in copies:
                copy.start()

    for x in range(ROWS):
        fields = jnp.concatenate([p[x], u[x + 1], v[x], w[x]], axis=0)
        cur[x] = fields
        feat_s[x] = fields.astype(BF16).astype(F32)

    def feature_copy(d):
        to = lax.rem(lev + d, levs)
        return pltpu.make_async_remote_copy(
            src_ref=feat_s.at[to], dst_ref=feat_r.at[lev], send_sem=feat_ss.at[d - 1], recv_sem=feat_rs.at[d - 1],
            device_id=(tile, to), device_id_type=MESH,
        )

    sends = [feature_copy(d) for d in range(1, levs)]
    for copy in sends:
        copy.start()
    fl[...] = jnp.zeros_like(fl)
    feat_r[lev] = feat_s[lev]
    for copy in sends:
        copy.wait()
    for s in range(levs):
        for f in range(4):
            a = feat_r[s, KL * f : KL * f + KL]
            fm[f, KL * s : KL * s + KL] = a
            fl[KL * s : KL * s + KL, f, :] = a

    @pl.loop(0, LEVELS, step=4)
    def _(l):
        for b in range(4):
            key_pass(l + b, fl, lk, rk, rs, eq)

    def tendency_copy(d):
        to = lax.rem(lev + d, levs)
        return pltpu.make_async_remote_copy(
            src_ref=tend_s.at[to], dst_ref=tend_r.at[lev], send_sem=tend_ss.at[d - 1], recv_sem=tend_rs.at[d - 1],
            device_id=(tile, to), device_id_type=MESH,
        )

    for d in range(1, levs + 1):
        to = lax.rem(lev + d, levs)

        @pl.loop(0, KL, step=2)
        def _(k):
            query_pass(to * KL + k, fl, fm, bias, ls, lf, tcol, rk, rs, eq, ot)

        for f in range(4):
            tend_s[to, KL * f : KL * f + KL] = ot[pl.ds(pl.multiple_of(to * KL, KL), KL), f, :]
        if d < levs:
            tendency_copy(d).start()

    tend_r[lev] = tend_s[lev]
    for d in range(1, levs):
        tendency_copy(d).wait()
    for x in range(ROWS):
        for f in range(4):
            rows = slice(KL * f, KL * f + KL)
            out[pl.ds(f * KL * ROWS + x, KL, stride=ROWS), :] = cur[x, rows] + tend_r[x, rows]


def shards(state, coef_x, coef_y, coef_z, slope, compress, ground, w_in, level_table, gain_attn,
           w_query, w_key, w_value, w_mix, temper, gain_head, w_tend):
    tiles, levs = lax.axis_size("tile"), lax.axis_size("lev")
    vmem = pl.BlockSpec(memory_space=pltpu.VMEM)
    smem = pl.BlockSpec(memory_space=pltpu.SMEM)
    hbm = pl.BlockSpec(memory_space=pl.ANY)
    dma = pltpu.SemaphoreType.DMA

    def buf(*shape, dtype=F32):
        return pltpu.VMEM(shape, dtype)

    def pair(*shape):
        return [buf(*shape), buf(*shape)]

    flat = KL * ROWS
    result = pl.pallas_call(
        lambda *refs: whole(tiles, levs, *refs),
        out_shape=jax.ShapeDtypeStruct((4 * flat, CELLS), F32),
        in_specs=[vmem] * 7 + [smem] + [vmem] * 5 + [hbm] * 4,
        out_specs=vmem,
        scratch_shapes=[
            buf(LEVELS, 8, CELLS), buf(LEVELS, 8, CELLS),
            buf(48, 128, dtype=BF16), buf(368, 128, dtype=BF16), buf(528, 640, dtype=BF16),
            buf(8, 128), buf(HEADS, LEVELS, CELLS), buf(LEVELS, CELLS), buf(LEVELS, CELLS), buf(LEVELS, CELLS),
            buf(4, LEVELS, CELLS),
            *[buf(WIDTH, WIDTH, dtype=BF16)] * 4, dma((4,)),
            *pair(4 * KL, CELLS), *pair(2, KL, CELLS), *pair(3, KL, CELLS),
            *pair(3 * ROWS, CELLS), *pair(2, ROWS, CELLS), *pair(3, ROWS, CELLS),
            *pair(3, 1, CELLS), *pair(3, 1, CELLS), dma((3, 6)), dma((3, 6)),
            *pair(levs, 4 * KL, CELLS), dma((levs - 1,)), dma((levs - 1,)),
            *pair(levs, 4 * KL, CELLS), dma((levs - 1,)), dma((levs - 1,)),
            buf(ROWS, 4 * KL, CELLS),
        ],
        compiler_params=pltpu.CompilerParams(
            collective_id=0, has_side_effects=True, vmem_limit_bytes=40 * 2**20
        ),
        name="substeps_and_columns",
    )(state.reshape(4 * flat, CELLS), *[a.reshape(flat, CELLS) for a in (coef_x, coef_y, coef_z, slope, compress)],
      ground, temper, w_in, level_table, gain_attn.reshape(1, WIDTH), gain_head.reshape(1, WIDTH), w_tend.T,
      w_query, w_key, w_value, w_mix)
    return result.reshape(4, KL, ROWS, CELLS)


def solution(mesh):
    block = P("lev", "tile", None)
    placed = (P(None, "lev", "tile", None),) + (block,) * 5 + (P("tile", None),) + (P(),) * 10
    return jax.shard_map(
        shards, mesh=mesh, in_specs=placed, out_specs=P(None, "lev", "tile", None), check_vma=False
    )
```

time: 261 us -> 60.5 us (0.23)
  the two profiles are of different devices: /device:TPU:7 before, /device:TPU:1 now
where the time goes in v1:
time: 60.5 us; the launch traced here: 59.8 us
  Pallas kernels  46.3 us (77%)
  local copies, waits for them, and re-layouts  13.5 us (22%)
    pallas_call x1, Pallas kernels, shards(): pl.pallas_call(lambda *refs: whole(tiles, levs, *refs), out_shape=jax.Sha...  46.3 us
    unnamed x35, local copies, waits for them, and re-layouts  13.5 us

profile of v1, /device:TPU:1, one launch (start us, length us, event | category | flops | bytes accessed | tf_op | source)
XLA Modules:
  0.0 59.8 jit_solution(14450724124407690617)
XLA Ops:
  0.0 0.0 copy-start.6
  0.0 0.0 copy-start.16
  0.0 0.7 %copy-done.6 = f32[8,4,128]{2,1,0:T(4,128)S(1)} copy-done((f32[8,4,128]{2,1,0:T(4,128)S(1)}, f32[8,4,128]{2,1,0:T(4,128)}, u32[]{:S(2)}) %copy-start.6) | copy-done | bytes 16408
  0.7 0.0 copy-done.16
  0.7 0.0 copy-start
  0.7 1.0 %copy-done = bf16[512,512]{1,0:T(8,128)(2,1)S(1)} copy-done((bf16[512,512]{1,0:T(8,128)(2,1)S(1)}, bf16[512,512]{1,0:T(8,128)(2,1)}, u32[]{:S(2)}) %copy-start) | copy-done | bytes 524312
  1.8 0.0 copy-start.1
  1.8 1.0 %copy-done.1 = bf16[512,512]{1,0:T(8,128)(2,1)S(1)} copy-done((bf16[512,512]{1,0:T(8,128)(2,1)S(1)}, bf16[512,512]{1,0:T(8,128)(2,1)}, u32[]{:S(2)}) %copy-start.1) | copy-done | bytes 524312
  2.8 0.0 copy-start.2
  2.8 1.0 %copy-done.2 = bf16[512,512]{1,0:T(8,128)(2,1)S(1)} copy-done((bf16[512,512]{1,0:T(8,128)(2,1)S(1)}, bf16[512,512]{1,0:T(8,128)(2,1)}, u32[]{:S(2)}) %copy-start.2) | copy-done | bytes 524312
  3.9 1.0 %copy-done.3 = bf16[512,512]{1,0:T(8,128)(2,1)S(1)} copy-done((bf16[512,512]{1,0:T(8,128)(2,1)S(1)}, bf16[512,512]{1,0:T(8,128)(2,1)}, u32[]{:S(2)}) %copy-start.3) | copy-done | bytes 524312
  4.9 0.8 %copy-done.4 = f32[4,8,4,128]{3,2,1,0:T(4,128)S(1)} copy-done((f32[4,8,4,128]{3,2,1,0:T(4,128)S(1)}, f32[4,8,4,128]{3,2,1,0:T(4,128)}, u32[]{:S(2)}) %copy-start.4) | copy-done | bytes 65560
  5.7 0.8 %copy-done.5 = f32[32,512]{1,0:T(8,128)S(1)} copy-done((f32[32,512]{1,0:T(8,128)S(1)}, f32[32,512]{1,0:T(8,128)}, u32[]{:S(2)}) %copy-start.5) | copy-done | bytes 65560
  6.6 0.7 %copy-done.7 = f32[8,4,128]{2,1,0:T(4,128)S(1)} copy-done((f32[8,4,128]{2,1,0:T(4,128)S(1)}, f32[8,4,128]{2,1,0:T(4,128)}, u32[]{:S(2)}) %copy-start.7) | copy-done | bytes 16408
  7.3 0.7 %copy-done.8 = f32[8,4,128]{2,1,0:T(4,128)S(1)} copy-done((f32[8,4,128]{2,1,0:T(4,128)S(1)}, f32[8,4,128]{2,1,0:T(4,128)}, u32[]{:S(2)}) %copy-start.8) | copy-done | bytes 16408
  8.0 0.7 %copy-done.9 = f32[8,4,128]{2,1,0:T(4,128)S(1)} copy-done((f32[8,4,128]{2,1,0:T(4,128)S(1)}, f32[8,4,128]{2,1,0:T(4,128)}, u32[]{:S(2)}) %copy-start.9) | copy-done | bytes 16408
  8.7 0.7 %copy-done.10 = f32[8,4,128]{2,1,0:T(4,128)S(1)} copy-done((f32[8,4,128]{2,1,0:T(4,128)S(1)}, f32[8,4,128]{2,1,0:T(4,128)}, u32[]{:S(2)}) %copy-start.10) | copy-done | bytes 16408
  9.4 0.7 %copy-done.11 = bf16[4,512]{1,0:T(4,128)(2,1)S(1)} copy-done((bf16[4,512]{1,0:T(4,128)(2,1)S(1)}, bf16[4,512]{1,0:T(4,128)(2,1)}, u32[]{:S(2)}) %copy-start.11) | copy-done | bytes 4120
  10.1 0.7 %copy-done.12 = bf16[512,4]{0,1:T(4,128)(2,1)S(1)} copy-done((bf16[512,4]{0,1:T(4,128)(2,1)S(1)}, bf16[512,4]{0,1:T(4,128)(2,1)}, u32[]{:S(2)}) %copy-start.12) | copy-done | bytes 4120
  10.8 0.7 %copy-done.13 = s32[4,128]{1,0:T(4,128)S(1)} copy-done((s32[4,128]{1,0:T(4,128)S(1)}, s32[4,128]{1,0:T(4,128)}, u32[]{:S(2)}) %copy-start.13) | copy-done | bytes 2072
  11.5 0.7 %copy-done.14 = f32[512]{0:T(512)S(1)} copy-done((f32[512]{0:T(512)S(1)}, f32[512]{0:T(512)}, u32[]{:S(2)}) %copy-start.14) | copy-done | bytes 2072
  12.2 0.7 %copy-done.15 = f32[512]{0:T(512)S(1)} copy-done((f32[512]{0:T(512)S(1)}, f32[512]{0:T(512)}, u32[]{:S(2)}) %copy-start.15) | copy-done | bytes 2072
  12.9 46.3 %substeps_and_columns.1 = f32[128,128]{1,0:T(8,128)S(1)} custom-call(f32[128,128]{1,0:T(8,128)S(1)} %bitcast.11, f32[32,128]{1,0:T(8,128)S(1)} %bitcast.12, f32[32,128]{1,0:T(8,128)S(1)} %bitcast.13, f32[32,128]{1,0:T(8,128)S(1)} %bitcast.14, f32[32,128]{1,0:T(8,128)S(1)} %bitcast.15, f32[32,128]{1,0:T(8,128)S(1)} %bitcast.16, s32[4,128]{1,0:T(4,128)S(1)} %copy-done.13, ...), custom_call_target="tpu_custom_call" | custom-call | tf_op jit(solution)/shard_map/substeps_and_columns/pallas_call | solution.py:374
  59.1 0.6 %copy.19 = f32[4,8,4,128]{3,2,1,0:T(4,128)} copy(f32[4,8,4,128]{3,2,1,0:T(4,128)S(1)} %bitcast.10) | data formatting | bytes 131072
  (12 shorter events, 0.0 us)
Async XLA Ops:
  0.0 0.7 %copy-start.6 = (f32[8,4,128]{2,1,0:T(4,128)S(1)}, f32[8,4,128]{2,1,0:T(4,128)}, u32[]{:S(2)}) copy-start(f32[8,4,128]{2,1,0:T(4,128)} %param.18) | copy-start | bytes 49156
  0.0 0.7 %copy-start.16 = (f32[8]{0:T(128)S(1)}, f32[8]{0:T(128)}, u32[]{:S(2)}) copy-start(f32[8]{0:T(128)} %refs_7_.1) | copy-start | bytes 100
  0.7 1.0 %copy-start = (bf16[512,512]{1,0:T(8,128)(2,1)S(1)}, bf16[512,512]{1,0:T(8,128)(2,1)}, u32[]{:S(2)}) copy-start(bf16[512,512]{1,0:T(8,128)(2,1)} %refs_13_.1) | copy-start | bytes 1572868
  1.8 1.0 %copy-start.1 = (bf16[512,512]{1,0:T(8,128)(2,1)S(1)}, bf16[512,512]{1,0:T(8,128)(2,1)}, u32[]{:S(2)}) copy-start(bf16[512,512]{1,0:T(8,128)(2,1)} %refs_14_.1) | copy-start | bytes 1572868
  2.8 1.0 %copy-start.2 = (bf16[512,512]{1,0:T(8,128)(2,1)S(1)}, bf16[512,512]{1,0:T(8,128)(2,1)}, u32[]{:S(2)}) copy-start(bf16[512,512]{1,0:T(8,128)(2,1)} %refs_15_.1) | copy-start | bytes 1572868
  3.8 1.0 %copy-start.3 = (bf16[512,512]{1,0:T(8,128)(2,1)S(1)}, bf16[512,512]{1,0:T(8,128)(2,1)}, u32[]{:S(2)}) copy-start(bf16[512,512]{1,0:T(8,128)(2,1)} %refs_16_.1) | copy-start | bytes 1572868
  4.9 0.8 %copy-start.4 = (f32[4,8,4,128]{3,2,1,0:T(4,128)S(1)}, f32[4,8,4,128]{3,2,1,0:T(4,128)}, u32[]{:S(2)}) copy-start(f32[4,8,4,128]{3,2,1,0:T(4,128)} %param.17) | copy-start | bytes 196612
  5.7 0.8 %copy-start.5 = (f32[32,512]{1,0:T(8,128)S(1)}, f32[32,512]{1,0:T(8,128)}, u32[]{:S(2)}) copy-start(f32[32,512]{1,0:T(8,128)} %refs_9_.1) | copy-start | bytes 196612
  6.6 0.7 %copy-start.7 = (f32[8,4,128]{2,1,0:T(4,128)S(1)}, f32[8,4,128]{2,1,0:T(4,128)}, u32[]{:S(2)}) copy-start(f32[8,4,128]{2,1,0:T(4,128)} %param.19) | copy-start | bytes 49156
  7.3 0.7 %copy-start.8 = (f32[8,4,128]{2,1,0:T(4,128)S(1)}, f32[8,4,128]{2,1,0:T(4,128)}, u32[]{:S(2)}) copy-start(f32[8,4,128]{2,1,0:T(4,128)} %param.20) | copy-start | bytes 49156
  8.0 0.7 %copy-start.9 = (f32[8,4,128]{2,1,0:T(4,128)S(1)}, f32[8,4,128]{2,1,0:T(4,128)}, u32[]{:S(2)}) copy-start(f32[8,4,128]{2,1,0:T(4,128)} %param.21) | copy-start | bytes 49156
  8.7 0.7 %copy-start.10 = (f32[8,4,128]{2,1,0:T(4,128)S(1)}, f32[8,4,128]{2,1,0:T(4,128)}, u32[]{:S(2)}) copy-start(f32[8,4,128]{2,1,0:T(4,128)} %param.22) | copy-start | bytes 49156
  9.4 0.7 %copy-start.11 = (bf16[4,512]{1,0:T(4,128)(2,1)S(1)}, bf16[4,512]{1,0:T(4,128)(2,1)}, u32[]{:S(2)}) copy-start(bf16[4,512]{1,0:T(4,128)(2,1)} %refs_8_.1) | copy-start | bytes 12292
  10.1 0.7 %copy-start.12 = (bf16[512,4]{0,1:T(4,128)(2,1)S(1)}, bf16[512,4]{0,1:T(4,128)(2,1)}, u32[]{:S(2)}) copy-start(bf16[512,4]{0,1:T(4,128)(2,1)} %param.33) | copy-start | bytes 12292
  10.8 0.7 %copy-start.13 = (s32[4,128]{1,0:T(4,128)S(1)}, s32[4,128]{1,0:T(4,128)}, u32[]{:S(2)}) copy-start(s32[4,128]{1,0:T(4,128)} %refs_6_.1) | copy-start | bytes 6148
  11.5 0.7 %copy-start.14 = (f32[512]{0:T(512)S(1)}, f32[512]{0:T(512)}, u32[]{:S(2)}) copy-start(f32[512]{0:T(512)} %param.26) | copy-start | bytes 6148
  12.2 0.7 %copy-start.15 = (f32[512]{0:T(512)S(1)}, f32[512]{0:T(512)}, u32[]{:S(2)}) copy-start(f32[512]{0:T(512)} %param.32) | copy-start | bytes 6148

commit v2 on v1

v2 whole, which is shorter than its diff:
```python
import math

import jax
import jax.numpy as jnp
from jax import lax
from jax.experimental import pallas as pl
from jax.experimental.pallas import tpu as pltpu
from jax.sharding import PartitionSpec as P

EPS = 1e-6
F32, BF16 = jnp.float32, jnp.bfloat16
LOG2E = math.log2(math.e)
HEADS, WIDTH, LEVELS, CELLS = 8, 512, 32, 128
HS = WIDTH // HEADS
X = 40


def dot(a, b):
    return jnp.dot(a, b, preferred_element_type=F32)


def dot_t(a, b):
    return lax.dot_general(a, b, (((1,), (1,)), ((), ())), precision=lax.Precision.HIGHEST, preferred_element_type=F32)


def split3(a):
    hi = a.astype(BF16).astype(F32)
    mid = (a - hi).astype(BF16).astype(F32)
    return hi, mid, a - hi - mid


def spread(a):
    hi, mid, lo = split3(a)
    return (hi + pltpu.roll(mid, X, 1) + pltpu.roll(lo, 2 * X, 1)).astype(BF16)


def prepare_maps(w_in, table, gain_attn, wq, wk, wv, wm, gain_head, w_tend, temper, lk, ls, lf, tcol):
    emb = jnp.concatenate([w_in[...].astype(F32), jnp.zeros((4, WIDTH), F32), table[...]], axis=0)
    xg3 = jnp.concatenate(split3(emb * gain_attn[...]), axis=0).astype(BF16)

    def through(w):
        a = dot(xg3, w[...])
        return a[:X] + a[X : 2 * X] + a[2 * X :]

    aq, ak, av = through(wq), through(wk), through(wv)
    pad = jnp.zeros((128 - X, WIDTH), F32)
    aq_p = jnp.concatenate([aq, pad], axis=0)
    ak_p = jnp.concatenate([ak, pad], axis=0)
    head = lax.broadcasted_iota(jnp.int32, (X, WIDTH), 1) // HS

    def by_head(a):
        return jnp.concatenate([jnp.where(head == h, a, 0.0) for h in range(HEADS)], axis=0)

    kb = by_head(ak)
    qb = by_head(aq)
    s_map = dot_t(kb, aq_p)
    kk = dot_t(kb, ak_p)
    qq = dot_t(qb, aq_p)
    ee = dot_t(emb, jnp.concatenate([emb, pad], axis=0))
    lane = lax.broadcasted_iota(jnp.int32, (1, 128), 1)
    twice = jnp.where(lane < 8, 1.0, 2.0)
    r40 = lax.broadcasted_iota(jnp.int32, (X, 128), 0)
    l40 = lax.broadcasted_iota(jnp.int32, (X, 128), 1)
    diag = (r40 == l40) & (r40 >= 8)

    def norm_rows(g):
        return [g[i : i + 1] * twice for i in range(4)] + [jnp.sum(jnp.where(diag, g, 0.0), axis=0, keepdims=True)]

    def norm_map(gram):
        per = [norm_rows(gram[X * h : X * h + X]) for h in range(HEADS)]
        return jnp.concatenate([per[h][i] for i in range(5) for h in range(HEADS)], axis=0)

    e_rows = norm_rows(ee) + [jnp.zeros((3, 128), F32)]
    lk[...] = spread(jnp.concatenate([norm_map(kk)] + e_rows, axis=0))
    ls[0:320] = spread(s_map)
    ls[320:360] = spread(norm_map(qq))
    ls[360:368] = jnp.zeros((8, 128), BF16)

    vh, vm, _ = split3(by_head(av))
    c = dot(vh.astype(BF16), wm[...]) + dot(vm.astype(BF16), wm[...])
    eh, em, el = split3(emb)
    rows = [c[X * h + 8 : X * h + X] for h in range(HEADS)]
    rows += [jnp.broadcast_to(c[X * h + i : X * h + i + 1], (8, WIDTH)) for h in range(HEADS) for i in range(4)]
    rows += [eh, em, el, jnp.zeros((8, WIDTH), F32)]
    lft = jnp.concatenate(rows, axis=0)
    wt = jnp.concatenate([w_tend[...].astype(F32), jnp.zeros((12, WIDTH), F32)], axis=0) * gain_head[...]
    t = dot_t(wt, lft)
    th = t[:8].astype(BF16).astype(F32)
    lf[0:512] = lft.T.astype(BF16)
    lf[512:528] = jnp.concatenate([th, t[:8] - th], axis=0).astype(BF16)
    square = (HEADS, HEADS)
    on_diag = lax.broadcasted_iota(jnp.int32, square, 0) == lax.broadcasted_iota(jnp.int32, square, 1)
    scale = jnp.sum(jnp.where(on_diag, temper[...], 0.0), axis=1, keepdims=True) * (LOG2E / math.sqrt(HS))
    tcol[...] = jnp.broadcast_to(scale, (HEADS, 128))


def token_rows(fl, l):
    lev = lax.broadcasted_iota(jnp.int32, (LEVELS, CELLS), 0) == l
    one = jnp.concatenate([fl[l], lev.astype(F32)], axis=0)
    return jnp.concatenate([one, one, one, jnp.zeros((8, CELLS), F32)], axis=0).astype(BF16)


def norms_at(out, f, base, epsq, scale):
    n = out[base + 32 : base + 40]
    for i in range(4):
        n = n + f[i : i + 1] * out[base + 8 * i : base + 8 * i + 8]
    return lax.rsqrt(jnp.maximum(n, 0.0) * (1.0 / HS) + epsq) * scale


def key_pass(l, fl, lk, rk, rs, eq):
    out = dot(lk[...], token_rows(fl, l))
    f = fl[l]
    n = out[44:45]
    for i in range(4):
        n = n + f[i : i + 1] * out[40 + i : 41 + i]
    ms = jnp.maximum(n, 0.0) * (1.0 / WIDTH) + EPS
    rs[pl.ds(l, 1), :] = lax.rsqrt(ms)
    eq[pl.ds(l, 1), :] = EPS * ms
    rk[:, l, :] = norms_at(out, f, 0, EPS * ms, 1.0)


def query_pass(l0, fl, fm, bias, ls, lf, tcol, rk, rs, eq, ot):
    x = jnp.concatenate([token_rows(fl, l0), token_rows(fl, l0 + 1)], axis=1)
    out = dot(ls[...], x)
    parts = []
    for a in range(2):
        o = out[:, 128 * a : 128 * a + 128]
        rq = norms_at(o, fl[l0 + a], 320, eq[pl.ds(l0 + a, 1), :], tcol[...])
        probs, sums = [], []
        for h in range(HEADS):
            s = o[X * h + 8 : X * h + X]
            for i in range(4):
                s = s + fm[i] * o[X * h + i : X * h + i + 1]
            s = s * rk[h] * rq[h : h + 1] + bias[...]
            p = jnp.exp2(s - jnp.max(s, axis=0, keepdims=True))
            p = p * (1.0 / jnp.sum(p, axis=0, keepdims=True)) * rs[...]
            probs.append(p)
            for i in range(4):
                z = p * fm[i]
                sums.append(z[0:8] + z[8:16] + z[16:24] + z[24:32])
        parts.append(jnp.concatenate(probs + sums, axis=0).astype(BF16))
    rhs = jnp.concatenate([jnp.concatenate(parts, axis=1), x], axis=0)
    fin = dot(lf[...], rhs)
    stream = fin[:512]
    ms = jnp.mean(stream * stream, axis=0, keepdims=True)
    tend = (fin[512:520] + fin[520:528]) * lax.rsqrt(ms + EPS)
    ot[l0] = tend[:, :128]
    ot[l0 + 1] = tend[:, 128:]


ROWS = 4
KL = 8
MESH = pl.DeviceIdType.MESH


NAMES = ("p", "u", "v", "w", "cx", "cy", "cz", "sl", "cp")
EASTWARD = [(n, x) for n in NAMES for x in range(1 if n in ("p", "u", "cx", "sl") else 2, ROWS)]
WESTWARD = [(n, x) for n in NAMES for x in range(3 if n == "p" else 2)]
HALF = KL // 2
ROUTES = [(dx, dk) for dx in (1, -1, 0) for dk in (0, 1, -1) if (dx, dk) != (0, 0)]


def message_rows(dx, dk):
    if dx == 0:
        return len(NAMES) * HALF * ROWS
    slabs = len(EASTWARD if dx > 0 else WESTWARD)
    return -(-slabs * (HALF if dk else KL) // 16) * 16


def substep(n, p, u, v, w, cx, sl, cy, cz, cp):
    up = {x: pltpu.roll(a, 3 * KL - 1, 0) for x, a in p.items()}
    down = {x: pltpu.roll(a, 1, 0) for x, a in p.items()}
    u = {
        x: u[x] - cx[x] * (p[x + 1] - p[x]) - 0.5 * sl[x] * (up[x] - down[x])
        for x in range(n - 3, ROWS + 2 - n)
    }
    new_p, new_v, new_w = {}, {}, {}
    for x in range(n - 2, ROWS + 2 - n):
        c = p[x]
        wx = w[x] - cz[x] * (up[x] - c)
        vx = v[x] - cy[x] * (pltpu.roll(c, CELLS - 1, 1) - c)
        div = (u[x] - u[x - 1]) + (vx - pltpu.roll(vx, 1, 1)) + (wx - pltpu.roll(wx, 1, 0))
        new_p[x] = c - cp[x] * div
        new_v[x] = vx
        new_w[x] = wx
    return new_p, u, new_v, new_w


def whole(tiles, levs, *refs):
    hbm, out, held, in_sem, rest = refs[:17], refs[17], refs[18:35], refs[35], refs[36:]
    loads = [pltpu.make_async_copy(src, dst, in_sem.at[n]) for n, (src, dst) in enumerate(zip(hbm, held))]
    for copy in loads:
        copy.start()
    (state, coef_x, coef_y, coef_z, slope, compress, ground, temper, w_in, table, gain_attn, gain_head, w_tend,
     wq, wk, wv, wm) = held
    (fl, ot, lk, ls, lf, tcol, rk, rs, eq, bias, fm,
     halo_ss, halo_rs, feat_s, feat_r, feat_ss, feat_rs, tend_s, tend_r, tend_ss, tend_rs, cur) = rest[:22]
    halo_s, halo_r, wide = rest[22:30], rest[30:38], rest[38:46]
    tile, lev = lax.axis_index("tile"), lax.axis_index("lev")
    there = [
        (tile + dx >= 0) & (tile + dx < tiles) & (lev + dk >= 0) & (lev + dk < levs) for dx, dk in ROUTES
    ]
    source_there = [there[ROUTES.index((-dx, -dk))] for dx, dk in ROUTES]

    barrier = pltpu.get_barrier_semaphore()
    for d in range(1, levs):
        pl.semaphore_signal(barrier, inc=1, device_id=(tile, lax.rem(lev + d, levs)), device_id_type=MESH)
    for (dx, dk), exists in zip(ROUTES, there):
        if dx:
            @pl.when(exists)
            def _():
                pl.semaphore_signal(barrier, inc=1, device_id=(tile + dx, lev + dk), device_id_type=MESH)

    for copy in loads[:6]:
        copy.wait()
    held_by = dict(zip(NAMES, [(state, f) for f in range(4)] + [(a, 0) for a in (coef_x, coef_y, coef_z, slope, compress)]))

    def slab(name, x, k=0, count=KL):
        ref, f = held_by[name]
        return ref[pl.ds((f * KL + k) * ROWS + x, count, stride=ROWS), :]

    for i, (dx, dk) in enumerate(ROUTES):
        k = HALF if dk > 0 else 0
        if dx == 0:
            pieces = [ref[(f * KL + k) * ROWS : (f * KL + k + HALF) * ROWS, :] for ref, f in held_by.values()]
        else:
            pieces = [slab(n, x, k, HALF if dk else KL) for n, x in (EASTWARD if dx > 0 else WESTWARD)]
        extra = message_rows(dx, dk) - sum(a.shape[0] for a in pieces)
        if extra:
            pieces.append(jnp.zeros((extra, CELLS), F32))
        halo_s[i][...] = jnp.concatenate(pieces, axis=0).astype(BF16)

        @pl.when(jnp.logical_not(source_there[i]))
        def _():
            halo_r[i][...] = jnp.zeros_like(halo_r[i])

    def halo_copy(i):
        dx, dk = ROUTES[i]
        return pltpu.make_async_remote_copy(
            src_ref=halo_s[i], dst_ref=halo_r[i], send_sem=halo_ss.at[i], recv_sem=halo_rs.at[i],
            device_id=(tile + dx, lev + dk), device_id_type=MESH,
        )

    beside = [exists.astype(jnp.int32) for (dx, dk), exists in zip(ROUTES, there) if dx]
    pl.semaphore_wait(barrier, levs - 1 + sum(beside))
    for i, exists in enumerate(there):
        @pl.when(exists)
        def _():
            halo_copy(i).start()

    for copy in loads[6:]:
        copy.wait()
    m_level = lax.broadcasted_iota(jnp.int32, (LEVELS, CELLS), 0)
    bias[...] = jnp.where(m_level >= ground[pl.ds(lev, 1), :], 0.0, -1e30)
    prepare_maps(w_in, table, gain_attn, wq, wk, wv, wm, gain_head, w_tend, temper, lk, ls, lf, tcol)

    for i in range(len(ROUTES)):
        @pl.when(there[i])
        def _():
            halo_copy(i).wait_send()

        @pl.when(source_there[i])
        def _():
            halo_copy(i).wait_recv()

    got = {}
    for i, (dx, dk) in enumerate(ROUTES):
        rows = message_rows(dx, dk)
        wide[i][0:16] = jnp.zeros((16, CELLS), F32)
        wide[i][16 : 16 + rows] = halo_r[i][...].astype(F32)
        wide[i][16 + rows :] = jnp.zeros((16, CELLS), F32)
        got[dx, dk] = wide[i]

    def column(a, name, x):
        if 0 <= x < ROWS:
            mid = slab(name, x)
            at = 16 + HALF * ROWS * a + x
            lo = got[0, 1][pl.ds(at - HALF * ROWS, KL, stride=ROWS), :]
            hi = got[0, -1][pl.ds(at, KL, stride=ROWS), :]
        else:
            dx = 1 if x < 0 else -1
            n = (EASTWARD if x < 0 else WESTWARD).index((name, x + ROWS if x < 0 else x - ROWS))
            mid = got[dx, 0][16 + KL * n : 16 + KL * n + KL, :]
            lo = got[dx, 1][16 + HALF * (n - 1) : 16 + HALF * (n + 1), :]
            hi = got[dx, -1][16 + HALF * n : 16 + HALF * (n + 2), :]
        return jnp.concatenate([lo, mid, hi], axis=0)

    held_x = {n: [x for x in range(-3, 7) if 0 <= x < ROWS or (n, x + ROWS) in EASTWARD and x < 0 or (n, x - ROWS) in WESTWARD and x >= ROWS] for n in NAMES}
    field = {n: {x: column(a, n, x) for x in held_x[n]} for a, n in enumerate(NAMES)}
    p, u, v, w = field["p"], field["u"], field["v"], field["w"]
    for n in range(3):
        p, u, v, w = substep(n, p, u, v, w, *[field[m] for m in ("cx", "sl", "cy", "cz", "cp")])

    mid = slice(KL, 2 * KL)
    for x in range(ROWS):
        fields = jnp.concatenate([a[x][mid] for a in (p, u, v, w)], axis=0)
        cur[x] = fields
        feat_s[x] = fields.astype(BF16).astype(F32)

    def feature_copy(d):
        to = lax.rem(lev + d, levs)
        return pltpu.make_async_remote_copy(
            src_ref=feat_s.at[to], dst_ref=feat_r.at[lev], send_sem=feat_ss.at[d - 1], recv_sem=feat_rs.at[d - 1],
            device_id=(tile, to), device_id_type=MESH,
        )

    sends = [feature_copy(d) for d in range(1, levs)]
    for copy in sends:
        copy.start()
    fl[...] = jnp.zeros_like(fl)
    feat_r[lev] = feat_s[lev]
    with jax.named_scope("features_wait"):
        for copy in sends:
            copy.wait()
    for s in range(levs):
        for f in range(4):
            a = feat_r[s, KL * f : KL * f + KL]
            fm[f, KL * s : KL * s + KL] = a
            fl[KL * s : KL * s + KL, f, :] = a

    with jax.named_scope("keys"):
        @pl.loop(0, LEVELS, step=4)
        def _(l):
            for b in range(4):
                key_pass(l + b, fl, lk, rk, rs, eq)

    def tendency_copy(d):
        to = lax.rem(lev + d, levs)
        return pltpu.make_async_remote_copy(
            src_ref=tend_s.at[to], dst_ref=tend_r.at[lev], send_sem=tend_ss.at[d - 1], recv_sem=tend_rs.at[d - 1],
            device_id=(tile, to), device_id_type=MESH,
        )

    with jax.named_scope("queries"):
        for d in range(1, levs + 1):
            to = lax.rem(lev + d, levs)

            @pl.loop(0, KL, step=2)
            def _(k):
                query_pass(to * KL + k, fl, fm, bias, ls, lf, tcol, rk, rs, eq, ot)

            for f in range(4):
                tend_s[to, KL * f : KL * f + KL] = ot[pl.ds(pl.multiple_of(to * KL, KL), KL), f, :]
            if d < levs:
                tendency_copy(d).start()

    tend_r[lev] = tend_s[lev]
    with jax.named_scope("tendency_wait"):
        for d in range(1, levs):
            tendency_copy(d).wait()
    for x in range(ROWS):
        for f in range(4):
            rows = slice(KL * f, KL * f + KL)
            out[pl.ds(f * KL * ROWS + x, KL, stride=ROWS), :] = cur[x, rows] + tend_r[x, rows]


def shards(state, coef_x, coef_y, coef_z, slope, compress, ground, w_in, level_table, gain_attn,
           w_query, w_key, w_value, w_mix, temper, gain_head, w_tend):
    tiles, levs = lax.axis_size("tile"), lax.axis_size("lev")
    dma = pltpu.SemaphoreType.DMA

    def buf(*shape, dtype=F32):
        return pltpu.VMEM(shape, dtype)

    def pair(*shape):
        return [buf(*shape), buf(*shape)]

    flat = KL * ROWS
    operands = (
        state.reshape(4 * flat, CELLS), *[a.reshape(flat, CELLS) for a in (coef_x, coef_y, coef_z, slope, compress)],
        ground, temper.reshape(1, HEADS), w_in, level_table, gain_attn.reshape(1, WIDTH), gain_head.reshape(1, WIDTH),
        w_tend.T, w_query, w_key, w_value, w_mix,
    )
    result = pl.pallas_call(
        lambda *refs: whole(tiles, levs, *refs),
        out_shape=jax.ShapeDtypeStruct((4 * flat, CELLS), F32),
        in_specs=[pl.BlockSpec(memory_space=pl.ANY)] * len(operands),
        out_specs=pl.BlockSpec(memory_space=pltpu.VMEM),
        scratch_shapes=[
            *[buf(*a.shape, dtype=a.dtype) for a in operands], dma((len(operands),)),
            buf(LEVELS, 8, CELLS), buf(LEVELS, 8, CELLS),
            buf(48, 128, dtype=BF16), buf(368, 128, dtype=BF16), buf(528, 640, dtype=BF16),
            buf(8, 128), buf(HEADS, LEVELS, CELLS), buf(LEVELS, CELLS), buf(LEVELS, CELLS), buf(LEVELS, CELLS),
            buf(4, LEVELS, CELLS),
            dma((len(ROUTES),)), dma((len(ROUTES),)),
            *pair(levs, 4 * KL, CELLS), dma((levs - 1,)), dma((levs - 1,)),
            *pair(levs, 4 * KL, CELLS), dma((levs - 1,)), dma((levs - 1,)),
            buf(ROWS, 4 * KL, CELLS),
            *[buf(message_rows(*r), CELLS, dtype=BF16) for r in ROUTES] * 2,
            *[buf(message_rows(*r) + 32, CELLS) for r in ROUTES],
        ],
        compiler_params=pltpu.CompilerParams(
            collective_id=0, has_side_effects=True, vmem_limit_bytes=60 * 2**20
        ),
        name="substeps_and_columns",
    )(*operands)
    return result.reshape(4, KL, ROWS, CELLS)


def solution(mesh):
    block = P("lev", "tile", None)
    placed = (P(None, "lev", "tile", None),) + (block,) * 5 + (P("tile", None),) + (P(),) * 10
    return jax.shard_map(
        shards, mesh=mesh, in_specs=placed, out_specs=P(None, "lev", "tile", None), check_vma=False
    )
```

time: 60.5 us -> 35 us (0.58)
  the two profiles are of different devices: /device:TPU:1 before, /device:TPU:7 now
where the time goes in v2:
time: 35 us; the launch traced here: 34.8 us
  Pallas kernels  33.4 us (95%)
  local copies, waits for them, and re-layouts  1.47 us (4%)
    pallas_call x1, Pallas kernels, shards(): pl.pallas_call(lambda *refs: whole(tiles, levs, *refs), out_shape=jax.Sha...  33.4 us
    unnamed x1, local copies, waits for them, and re-layouts  1.47 us

profile of v2, /device:TPU:7, one launch (start us, length us, event | category | flops | bytes accessed | tf_op | source)
XLA Modules:
  0.0 34.8 jit_solution(12189505540995278287)
XLA Ops:
  0.0 33.4 %substeps_and_columns.1 = f32[128,128]{1,0:T(8,128)} custom-call(f32[128,128]{1,0:T(8,128)} %bitcast.12, f32[32,128]{1,0:T(8,128)} %bitcast.13, f32[32,128]{1,0:T(8,128)} %bitcast.14, f32[32,128]{1,0:T(8,128)} %bitcast.15, f32[32,128]{1,0:T(8,128)} %bitcast.16, f32[32,128]{1,0:T(8,128)} %bitcast.17, s32[4,128]{1,0:T(4,128)} %refs_6_.1, f32[1,8]{1,0:T(1,128)} %bitcast.21, ...), custom_call_target="tpu_custom_call" | custom-call | tf_op jit(solution)/shard_map/substeps_and_columns/pallas_call | solution.py:374
  33.4 1.5 %copy.19 = f32[4,8,4,128]{3,2,1,0:T(4,128)} copy(f32[4,8,4,128]{3,2,1,0:T(4,128)} %bitcast.11) | data formatting | bytes 131072

commit v3 on v2

--- a/solution.py
+++ b/solution.py
@@ -80,7 +80,7 @@
     c = dot(vh.astype(BF16), wm[...]) + dot(vm.astype(BF16), wm[...])
     eh, em, el = split3(emb)
     rows = [c[X * h + 8 : X * h + X] for h in range(HEADS)]
-    rows += [jnp.broadcast_to(c[X * h + i : X * h + i + 1], (8, WIDTH)) for h in range(HEADS) for i in range(4)]
+    rows += [jnp.broadcast_to(c[X * h + i : X * h + i + 1], (4, WIDTH)) for h in range(HEADS) for i in range(4)]
     rows += [eh, em, el, jnp.zeros((8, WIDTH), F32)]
     lft = jnp.concatenate(rows, axis=0)
     wt = jnp.concatenate([w_tend[...].astype(F32), jnp.zeros((12, WIDTH), F32)], axis=0) * gain_head[...]
@@ -107,22 +107,31 @@
     return lax.rsqrt(jnp.maximum(n, 0.0) * (1.0 / HS) + epsq) * scale
 
 
-def key_pass(l, fl, lk, rk, rs, eq):
-    out = dot(lk[...], token_rows(fl, l))
-    f = fl[l]
-    n = out[44:45]
-    for i in range(4):
-        n = n + f[i : i + 1] * out[40 + i : 41 + i]
-    ms = jnp.maximum(n, 0.0) * (1.0 / WIDTH) + EPS
-    rs[pl.ds(l, 1), :] = lax.rsqrt(ms)
-    eq[pl.ds(l, 1), :] = EPS * ms
-    rk[:, l, :] = norms_at(out, f, 0, EPS * ms, 1.0)
-
-
-def query_pass(l0, fl, fm, bias, ls, lf, tcol, rk, rs, eq, ot):
+def key_chunk(base, pairs, fl, lk, rk, rs, eq):
+    for l0 in [base + 2 * j for j in range(pairs)]:
+        x = jnp.concatenate([token_rows(fl, l0), token_rows(fl, l0 + 1)], axis=1)
+        both = dot(lk[...], x)
+        for a in range(2):
+            l = l0 + a
+            out = both[:, 128 * a : 128 * a + 128]
+            f = fl[l]
+            n = out[44:45]
+            for i in range(4):
+                n = n + f[i : i + 1] * out[40 + i : 41 + i]
+            ms = jnp.maximum(n, 0.0) * (1.0 / WIDTH) + EPS
+            rs[pl.ds(l, 1), :] = lax.rsqrt(ms)
+            eq[pl.ds(l, 1), :] = EPS * ms
+            rk[:, l, :] = norms_at(out, f, 0, EPS * ms, 1.0)
+
+
+def score_terms(l0, fl, ls):
     x = jnp.concatenate([token_rows(fl, l0), token_rows(fl, l0 + 1)], axis=1)
-    out = dot(ls[...], x)
+    return x, dot(ls[...], x)
+
+
+def attend(l0, x, out, fl, fm, bias, tcol, rk, rs, eq):
     parts = []
+    low = lax.broadcasted_iota(jnp.int32, (8, CELLS), 0) < 4
     for a in range(2):
         o = out[:, 128 * a : 128 * a + 128]
         rq = norms_at(o, fl[l0 + a], 320, eq[pl.ds(l0 + a, 1), :], tcol[...])
@@ -135,17 +144,34 @@
             p = jnp.exp2(s - jnp.max(s, axis=0, keepdims=True))
             p = p * (1.0 / jnp.sum(p, axis=0, keepdims=True)) * rs[...]
             probs.append(p)
-            for i in range(4):
-                z = p * fm[i]
-                sums.append(z[0:8] + z[8:16] + z[16:24] + z[24:32])
+            z = [p * fm[i] for i in range(4)]
+            z = [a[0:8] + a[8:16] + a[16:24] + a[24:32] for a in z]
+            for i in (0, 2):
+                sums.append(jnp.where(low, z[i], z[i + 1]) + pltpu.roll(jnp.where(low, z[i + 1], z[i]), 4, 0))
         parts.append(jnp.concatenate(probs + sums, axis=0).astype(BF16))
-    rhs = jnp.concatenate([jnp.concatenate(parts, axis=1), x], axis=0)
+    return jnp.concatenate([jnp.concatenate(parts, axis=1), x], axis=0)
+
+
+def finish(l0, rhs, lf, ot):
     fin = dot(lf[...], rhs)
     stream = fin[:512]
     ms = jnp.mean(stream * stream, axis=0, keepdims=True)
     tend = (fin[512:520] + fin[520:528]) * lax.rsqrt(ms + EPS)
     ot[l0] = tend[:, :128]
     ot[l0 + 1] = tend[:, 128:]
+
+
+def query_pairs(levels, fl, fm, bias, ls, lf, tcol, rk, rs, eq, ot, done=lambda n: None):
+    pairs = len(levels)
+    first, second = {}, {}
+    for step in range(pairs + 2):
+        if step < pairs:
+            first[step] = score_terms(levels[step], fl, ls)
+        if step >= 2:
+            finish(levels[step - 2], second.pop(step - 2), lf, ot)
+            done(step - 2)
+        if 1 <= step <= pairs:
+            second[step - 1] = attend(levels[step - 1], *first.pop(step - 1), fl, fm, bias, tcol, rk, rs, eq)
 
 
 ROWS = 4
@@ -188,9 +214,6 @@
 
 def whole(tiles, levs, *refs):
     hbm, out, held, in_sem, rest = refs[:17], refs[17], refs[18:35], refs[35], refs[36:]
-    loads = [pltpu.make_async_copy(src, dst, in_sem.at[n]) for n, (src, dst) in enumerate(zip(hbm, held))]
-    for copy in loads:
-        copy.start()
     (state, coef_x, coef_y, coef_z, slope, compress, ground, temper, w_in, table, gain_attn, gain_head, w_tend,
      wq, wk, wv, wm) = held
     (fl, ot, lk, ls, lf, tcol, rk, rs, eq, bias, fm,
@@ -211,6 +234,9 @@
             def _():
                 pl.semaphore_signal(barrier, inc=1, device_id=(tile + dx, lev + dk), device_id_type=MESH)
 
+    loads = [pltpu.make_async_copy(src, dst, in_sem.at[n]) for n, (src, dst) in enumerate(zip(hbm, held))]
+    for copy in loads:
+        copy.start()
     for copy in loads[:6]:
         copy.wait()
     held_by = dict(zip(NAMES, [(state, f) for f in range(4)] + [(a, 0) for a in (coef_x, coef_y, coef_z, slope, compress)]))
@@ -304,25 +330,23 @@
             device_id=(tile, to), device_id_type=MESH,
         )
 
-    sends = [feature_copy(d) for d in range(1, levs)]
-    for copy in sends:
-        copy.start()
+    for d in range(1, levs):
+        feature_copy(d).start()
     fl[...] = jnp.zeros_like(fl)
-    feat_r[lev] = feat_s[lev]
-    with jax.named_scope("features_wait"):
-        for copy in sends:
-            copy.wait()
-    for s in range(levs):
+
+    def take(features, s):
         for f in range(4):
-            a = feat_r[s, KL * f : KL * f + KL]
-            fm[f, KL * s : KL * s + KL] = a
-            fl[KL * s : KL * s + KL, f, :] = a
-
-    with jax.named_scope("keys"):
-        @pl.loop(0, LEVELS, step=4)
-        def _(l):
-            for b in range(4):
-                key_pass(l + b, fl, lk, rk, rs, eq)
+            a = features[KL * f : KL * f + KL]
+            at = pl.ds(pl.multiple_of(s * KL, KL), KL)
+            fm[f, at] = a
+            fl[at, f, :] = a
+        key_chunk(s * KL, KL // 2, fl, lk, rk, rs, eq)
+
+    take(feat_s[lev], lev)
+    for d in range(1, levs):
+        s = lax.rem(lev + levs - d, levs)
+        feature_copy(d).wait_recv()
+        take(feat_r[s], s)
 
     def tendency_copy(d):
         to = lax.rem(lev + d, levs)
@@ -331,23 +355,24 @@
             device_id=(tile, to), device_id_type=MESH,
         )
 
-    with jax.named_scope("queries"):
-        for d in range(1, levs + 1):
-            to = lax.rem(lev + d, levs)
-
-            @pl.loop(0, KL, step=2)
-            def _(k):
-                query_pass(to * KL + k, fl, fm, bias, ls, lf, tcol, rk, rs, eq, ot)
-
+    blocks = [lax.rem(lev + d, levs) for d in range(1, levs + 1)]
+
+    def done(n):
+        d, j = n // (KL // 2), n % (KL // 2)
+        if j == KL // 2 - 1:
+            to = blocks[d]
             for f in range(4):
                 tend_s[to, KL * f : KL * f + KL] = ot[pl.ds(pl.multiple_of(to * KL, KL), KL), f, :]
-            if d < levs:
-                tendency_copy(d).start()
-
+            if d < levs - 1:
+                tendency_copy(d + 1).start()
+
+    query_pairs(
+        [to * KL + k for to in blocks for k in range(0, KL, 2)], fl, fm, bias, ls, lf, tcol, rk, rs, eq, ot, done
+    )
     tend_r[lev] = tend_s[lev]
-    with jax.named_scope("tendency_wait"):
-        for d in range(1, levs):
-            tendency_copy(d).wait()
+    for d in range(1, levs):
+        feature_copy(d).wait_send()
+        tendency_copy(d).wait()
     for x in range(ROWS):
         for f in range(4):
             rows = slice(KL * f, KL * f + KL)
@@ -379,7 +404,7 @@
         scratch_shapes=[
             *[buf(*a.shape, dtype=a.dtype) for a in operands], dma((len(operands),)),
             buf(LEVELS, 8, CELLS), buf(LEVELS, 8, CELLS),
-            buf(48, 128, dtype=BF16), buf(368, 128, dtype=BF16), buf(528, 640, dtype=BF16),
+            buf(48, 128, dtype=BF16), buf(368, 128, dtype=BF16), buf(528, 512, dtype=BF16),
             buf(8, 128), buf(HEADS, LEVELS, CELLS), buf(LEVELS, CELLS), buf(LEVELS, CELLS), buf(LEVELS, CELLS),
             buf(4, LEVELS, CELLS),
             dma((len(ROUTES),)), dma((len(ROUTES),)),

time: 35 us -> 28.7 us (0.82)
  Pallas kernels: 33.4 us -> 27.1 us
    pallas_call x1, Pallas kernels: 33.4 us -> 27.1 us  [shards(): pl.pallas_call(lambda *refs: whole(tiles, levs, *refs), out_shape=jax.Sha...]
where the time goes in v3:
time: 28.7 us; the launch traced here: 28.6 us
  Pallas kernels  27.1 us (94%)
  local copies, waits for them, and re-layouts  1.47 us (5%)
    pallas_call x1, Pallas kernels, shards(): pl.pallas_call(lambda *refs: whole(tiles, levs, *refs), out_shape=jax.Sha...  27.1 us
    unnamed x1, local copies, waits for them, and re-layouts  1.47 us

profile of v3, /device:TPU:7, one launch (start us, length us, event | category | flops | bytes accessed | tf_op | source)
XLA Modules:
  0.0 28.6 jit_solution(15829302676074130859)
XLA Ops:
  0.0 27.1 %substeps_and_columns.1 = f32[128,128]{1,0:T(8,128)} custom-call(f32[128,128]{1,0:T(8,128)} %bitcast.12, f32[32,128]{1,0:T(8,128)} %bitcast.13, f32[32,128]{1,0:T(8,128)} %bitcast.14, f32[32,128]{1,0:T(8,128)} %bitcast.15, f32[32,128]{1,0:T(8,128)} %bitcast.16, f32[32,128]{1,0:T(8,128)} %bitcast.17, s32[4,128]{1,0:T(4,128)} %refs_6_.1, f32[1,8]{1,0:T(1,128)} %bitcast.21, ...), custom_call_target="tpu_custom_call" | custom-call | tf_op jit(solution)/shard_map/substeps_and_columns/pallas_call | solution.py:399
  27.1 1.5 %copy.19 = f32[4,8,4,128]{3,2,1,0:T(4,128)} copy(f32[4,8,4,128]{3,2,1,0:T(4,128)} %bitcast.11) | data formatting | bytes 131072

commit v4 on v3

--- a/solution.py
+++ b/solution.py
@@ -220,19 +220,21 @@
      halo_ss, halo_rs, feat_s, feat_r, feat_ss, feat_rs, tend_s, tend_r, tend_ss, tend_rs, cur) = rest[:22]
     halo_s, halo_r, wide = rest[22:30], rest[30:38], rest[38:46]
     tile, lev = lax.axis_index("tile"), lax.axis_index("lev")
+    near = lev + 1 - 2 * lax.rem(lev, 2)
+    peers = [near, lax.rem(lev + 2, levs), lax.rem(near + 2, levs)]
     there = [
         (tile + dx >= 0) & (tile + dx < tiles) & (lev + dk >= 0) & (lev + dk < levs) for dx, dk in ROUTES
     ]
     source_there = [there[ROUTES.index((-dx, -dk))] for dx, dk in ROUTES]
 
     barrier = pltpu.get_barrier_semaphore()
-    for d in range(1, levs):
-        pl.semaphore_signal(barrier, inc=1, device_id=(tile, lax.rem(lev + d, levs)), device_id_type=MESH)
     for (dx, dk), exists in zip(ROUTES, there):
         if dx:
             @pl.when(exists)
             def _():
                 pl.semaphore_signal(barrier, inc=1, device_id=(tile + dx, lev + dk), device_id_type=MESH)
+    for to in peers:
+        pl.semaphore_signal(barrier, inc=1, device_id=(tile, to), device_id_type=MESH)
 
     loads = [pltpu.make_async_copy(src, dst, in_sem.at[n]) for n, (src, dst) in enumerate(zip(hbm, held))]
     for copy in loads:
@@ -321,41 +323,41 @@
     for x in range(ROWS):
         fields = jnp.concatenate([a[x][mid] for a in (p, u, v, w)], axis=0)
         cur[x] = fields
-        feat_s[x] = fields.astype(BF16).astype(F32)
-
-    def feature_copy(d):
-        to = lax.rem(lev + d, levs)
+        feat_s[x] = fields.astype(BF16)
+
+    def feature_copy(n):
+        to = peers[n]
         return pltpu.make_async_remote_copy(
-            src_ref=feat_s.at[to], dst_ref=feat_r.at[lev], send_sem=feat_ss.at[d - 1], recv_sem=feat_rs.at[d - 1],
+            src_ref=feat_s.at[to], dst_ref=feat_r.at[lev], send_sem=feat_ss.at[n], recv_sem=feat_rs.at[n],
             device_id=(tile, to), device_id_type=MESH,
         )
 
-    for d in range(1, levs):
-        feature_copy(d).start()
+    for n in (1, 2, 0):
+        feature_copy(n).start()
     fl[...] = jnp.zeros_like(fl)
 
     def take(features, s):
         for f in range(4):
-            a = features[KL * f : KL * f + KL]
+            a = features[KL * f : KL * f + KL].astype(F32)
             at = pl.ds(pl.multiple_of(s * KL, KL), KL)
             fm[f, at] = a
             fl[at, f, :] = a
         key_chunk(s * KL, KL // 2, fl, lk, rk, rs, eq)
 
     take(feat_s[lev], lev)
-    for d in range(1, levs):
-        s = lax.rem(lev + levs - d, levs)
-        feature_copy(d).wait_recv()
+    for n, s in enumerate(peers):
+        feature_copy(n).wait_recv()
         take(feat_r[s], s)
 
-    def tendency_copy(d):
-        to = lax.rem(lev + d, levs)
+    def tendency_copy(n):
+        to = peers[n]
         return pltpu.make_async_remote_copy(
-            src_ref=tend_s.at[to], dst_ref=tend_r.at[lev], send_sem=tend_ss.at[d - 1], recv_sem=tend_rs.at[d - 1],
+            src_ref=tend_s.at[to], dst_ref=tend_r.at[lev], send_sem=tend_ss.at[n], recv_sem=tend_rs.at[n],
             device_id=(tile, to), device_id_type=MESH,
         )
 
-    blocks = [lax.rem(lev + d, levs) for d in range(1, levs + 1)]
+    turns = (1, 2, 0)
+    blocks = [peers[n] for n in turns] + [lev]
 
     def done(n):
         d, j = n // (KL // 2), n % (KL // 2)
@@ -364,15 +366,15 @@
             for f in range(4):
                 tend_s[to, KL * f : KL * f + KL] = ot[pl.ds(pl.multiple_of(to * KL, KL), KL), f, :]
             if d < levs - 1:
-                tendency_copy(d + 1).start()
+                tendency_copy(turns[d]).start()
 
     query_pairs(
         [to * KL + k for to in blocks for k in range(0, KL, 2)], fl, fm, bias, ls, lf, tcol, rk, rs, eq, ot, done
     )
     tend_r[lev] = tend_s[lev]
-    for d in range(1, levs):
-        feature_copy(d).wait_send()
-        tendency_copy(d).wait()
+    for n in range(levs - 1):
+        feature_copy(n).wait_send()
+        tendency_copy(n).wait()
     for x in range(ROWS):
         for f in range(4):
             rows = slice(KL * f, KL * f + KL)
@@ -408,7 +410,7 @@
             buf(8, 128), buf(HEADS, LEVELS, CELLS), buf(LEVELS, CELLS), buf(LEVELS, CELLS), buf(LEVELS, CELLS),
             buf(4, LEVELS, CELLS),
             dma((len(ROUTES),)), dma((len(ROUTES),)),
-            *pair(levs, 4 * KL, CELLS), dma((levs - 1,)), dma((levs - 1,)),
+            *[buf(levs, 4 * KL, CELLS, dtype=BF16)] * 2, dma((levs - 1,)), dma((levs - 1,)),
             *pair(levs, 4 * KL, CELLS), dma((levs - 1,)), dma((levs - 1,)),
             buf(ROWS, 4 * KL, CELLS),
             *[buf(message_rows(*r), CELLS, dtype=BF16) for r in ROUTES] * 2,

time: 28.7 us -> 26.9 us (0.937)
  Pallas kernels: 27.1 us -> 25.2 us
    pallas_call x1, Pallas kernels: 27.1 us -> 25.2 us  [shards(): pl.pallas_call(lambda *refs: whole(tiles, levs, *refs), out_shape=jax.Sha...]
where the time goes in v4:
time: 26.9 us; the launch traced here: 26.7 us
  Pallas kernels  25.2 us (94%)
  local copies, waits for them, and re-layouts  1.47 us (5%)
    pallas_call x1, Pallas kernels, shards(): pl.pallas_call(lambda *refs: whole(tiles, levs, *refs), out_shape=jax.Sha...  25.2 us
    unnamed x1, local copies, waits for them, and re-layouts  1.47 us

profile of v4, /device:TPU:7, one launch (start us, length us, event | category | flops | bytes accessed | tf_op | source)
XLA Modules:
  0.0 26.7 jit_solution(12715520652408203911)
XLA Ops:
  0.0 25.2 %substeps_and_columns.1 = f32[128,128]{1,0:T(8,128)} custom-call(f32[128,128]{1,0:T(8,128)} %bitcast.12, f32[32,128]{1,0:T(8,128)} %bitcast.13, f32[32,128]{1,0:T(8,128)} %bitcast.14, f32[32,128]{1,0:T(8,128)} %bitcast.15, f32[32,128]{1,0:T(8,128)} %bitcast.16, f32[32,128]{1,0:T(8,128)} %bitcast.17, s32[4,128]{1,0:T(4,128)} %refs_6_.1, f32[1,8]{1,0:T(1,128)} %bitcast.21, ...), custom_call_target="tpu_custom_call" | custom-call | tf_op jit(solution)/shard_map/substeps_and_columns/pallas_call | solution.py:401
  25.2 1.5 %copy.19 = f32[4,8,4,128]{3,2,1,0:T(4,128)} copy(f32[4,8,4,128]{3,2,1,0:T(4,128)} %bitcast.11) | data formatting | bytes 131072

commit v5 on v4

--- a/solution.py
+++ b/solution.py
@@ -182,15 +182,25 @@
 NAMES = ("p", "u", "v", "w", "cx", "cy", "cz", "sl", "cp")
 EASTWARD = [(n, x) for n in NAMES for x in range(1 if n in ("p", "u", "cx", "sl") else 2, ROWS)]
 WESTWARD = [(n, x) for n in NAMES for x in range(3 if n == "p" else 2)]
-HALF = KL // 2
 ROUTES = [(dx, dk) for dx in (1, -1, 0) for dk in (0, 1, -1) if (dx, dk) != (0, 0)]
-
-
-def message_rows(dx, dk):
+MARGIN = 32
+
+
+def slots(dx, dk):
+    tall = ("p", "w", "cz")
     if dx == 0:
-        return len(NAMES) * HALF * ROWS
-    slabs = len(EASTWARD if dx > 0 else WESTWARD)
-    return -(-slabs * (HALF if dk else KL) // 16) * 16
+        wanted = [((n, None), 3 if n in tall else 2) for n in NAMES]
+    elif dk == 0:
+        wanted = [(s, KL) for s in (EASTWARD if dx > 0 else WESTWARD)]
+    elif dx > 0:
+        wanted = [(s, 3 if s[0] == "p" or s[0] in tall and dk > 0 else 2) for s in EASTWARD]
+    else:
+        wanted = [((n, x), 2 - x if n in tall else 1) for n in NAMES for x in range(2 if n in tall else 1)]
+    table, row = {}, 0
+    for key, levels in wanted:
+        table[key] = row, levels
+        row += levels * (ROWS if dx == 0 else 1)
+    return table, -(-row // 16) * 16
 
 
 def substep(n, p, u, v, w, cx, sl, cy, cz, cp):
@@ -248,12 +258,16 @@
         return ref[pl.ds((f * KL + k) * ROWS + x, count, stride=ROWS), :]
 
     for i, (dx, dk) in enumerate(ROUTES):
-        k = HALF if dk > 0 else 0
-        if dx == 0:
-            pieces = [ref[(f * KL + k) * ROWS : (f * KL + k + HALF) * ROWS, :] for ref, f in held_by.values()]
-        else:
-            pieces = [slab(n, x, k, HALF if dk else KL) for n, x in (EASTWARD if dx > 0 else WESTWARD)]
-        extra = message_rows(dx, dk) - sum(a.shape[0] for a in pieces)
+        layout, rows = slots(dx, dk)
+        pieces = []
+        for (name, x), (_, levels) in layout.items():
+            k = KL - levels if dk > 0 else 0
+            if dx == 0:
+                ref, f = held_by[name]
+                pieces.append(ref[(f * KL + k) * ROWS : (f * KL + k + levels) * ROWS, :])
+            else:
+                pieces.append(slab(name, x, k, levels))
+        extra = rows - sum(a.shape[0] for a in pieces)
         if extra:
             pieces.append(jnp.zeros((extra, CELLS), F32))
         halo_s[i][...] = jnp.concatenate(pieces, axis=0).astype(BF16)
@@ -293,28 +307,31 @@
 
     got = {}
     for i, (dx, dk) in enumerate(ROUTES):
-        rows = message_rows(dx, dk)
-        wide[i][0:16] = jnp.zeros((16, CELLS), F32)
-        wide[i][16 : 16 + rows] = halo_r[i][...].astype(F32)
-        wide[i][16 + rows :] = jnp.zeros((16, CELLS), F32)
+        rows = slots(dx, dk)[1]
+        wide[i][0:MARGIN] = jnp.zeros((MARGIN, CELLS), F32)
+        wide[i][MARGIN : MARGIN + rows] = halo_r[i][...].astype(F32)
+        wide[i][MARGIN + rows :] = jnp.zeros((MARGIN, CELLS), F32)
         got[dx, dk] = wide[i]
 
-    def column(a, name, x):
-        if 0 <= x < ROWS:
-            mid = slab(name, x)
-            at = 16 + HALF * ROWS * a + x
-            lo = got[0, 1][pl.ds(at - HALF * ROWS, KL, stride=ROWS), :]
-            hi = got[0, -1][pl.ds(at, KL, stride=ROWS), :]
-        else:
-            dx = 1 if x < 0 else -1
-            n = (EASTWARD if x < 0 else WESTWARD).index((name, x + ROWS if x < 0 else x - ROWS))
-            mid = got[dx, 0][16 + KL * n : 16 + KL * n + KL, :]
-            lo = got[dx, 1][16 + HALF * (n - 1) : 16 + HALF * (n + 1), :]
-            hi = got[dx, -1][16 + HALF * n : 16 + HALF * (n + 2), :]
-        return jnp.concatenate([lo, mid, hi], axis=0)
+    def column(name, x):
+        dx = 1 if x < 0 else -1 if x >= ROWS else 0
+        key = (name, x + ROWS * dx if dx else None)
+        parts = []
+        for dk in (1, 0, -1):
+            if dx == 0 and dk == 0:
+                parts.append(slab(name, x))
+                continue
+            first, levels = slots(dx, dk)[0].get(key, (None, 0))
+            if levels == 0:
+                parts.append(jnp.zeros((KL, CELLS), F32))
+                continue
+            stride = 1 if dx else ROWS
+            at = MARGIN + first - (stride * (KL - levels) if dk > 0 else 0) + (0 if dx else x)
+            parts.append(got[dx, dk][pl.ds(at, KL, stride=stride) if stride > 1 else slice(at, at + KL), :])
+        return jnp.concatenate(parts, axis=0)
 
     held_x = {n: [x for x in range(-3, 7) if 0 <= x < ROWS or (n, x + ROWS) in EASTWARD and x < 0 or (n, x - ROWS) in WESTWARD and x >= ROWS] for n in NAMES}
-    field = {n: {x: column(a, n, x) for x in held_x[n]} for a, n in enumerate(NAMES)}
+    field = {n: {x: column(n, x) for x in held_x[n]} for n in NAMES}
     p, u, v, w = field["p"], field["u"], field["v"], field["w"]
     for n in range(3):
         p, u, v, w = substep(n, p, u, v, w, *[field[m] for m in ("cx", "sl", "cy", "cz", "cp")])
@@ -413,8 +430,8 @@
             *[buf(levs, 4 * KL, CELLS, dtype=BF16)] * 2, dma((levs - 1,)), dma((levs - 1,)),
             *pair(levs, 4 * KL, CELLS), dma((levs - 1,)), dma((levs - 1,)),
             buf(ROWS, 4 * KL, CELLS),
-            *[buf(message_rows(*r), CELLS, dtype=BF16) for r in ROUTES] * 2,
-            *[buf(message_rows(*r) + 32, CELLS) for r in ROUTES],
+            *[buf(slots(*r)[1], CELLS, dtype=BF16) for r in ROUTES] * 2,
+            *[buf(slots(*r)[1] + 2 * MARGIN, CELLS) for r in ROUTES],
         ],
         compiler_params=pltpu.CompilerParams(
             collective_id=0, has_side_effects=True, vmem_limit_bytes=60 * 2**20

time: 26.9 us -> 26.7 us (level)
  no operation moved by 1% of the time
where the time goes in v5:
time: 26.7 us; the launch traced here: 26.5 us
  Pallas kernels  25.1 us (94%)
  local copies, waits for them, and re-layouts  1.47 us (6%)
    pallas_call x1, Pallas kernels, shards(): pl.pallas_call(lambda *refs: whole(tiles, levs, *refs), out_shape=jax.Sha...  25.1 us
    unnamed x1, local copies, waits for them, and re-layouts  1.47 us

profile of v5, /device:TPU:7, one launch (start us, length us, event | category | flops | bytes accessed | tf_op | source)
XLA Modules:
  0.0 26.5 jit_solution(12505290324326446835)
XLA Ops:
  0.0 25.1 %substeps_and_columns.1 = f32[128,128]{1,0:T(8,128)} custom-call(f32[128,128]{1,0:T(8,128)} %bitcast.12, f32[32,128]{1,0:T(8,128)} %bitcast.13, f32[32,128]{1,0:T(8,128)} %bitcast.14, f32[32,128]{1,0:T(8,128)} %bitcast.15, f32[32,128]{1,0:T(8,128)} %bitcast.16, f32[32,128]{1,0:T(8,128)} %bitcast.17, s32[4,128]{1,0:T(4,128)} %refs_6_.1, f32[1,8]{1,0:T(1,128)} %bitcast.21, ...), custom_call_target="tpu_custom_call" | custom-call | tf_op jit(solution)/shard_map/substeps_and_columns/pallas_call | solution.py:418
  25.1 1.5 %copy.19 = f32[4,8,4,128]{3,2,1,0:T(4,128)} copy(f32[4,8,4,128]{3,2,1,0:T(4,128)} %bitcast.11) | data formatting | bytes 131072

commit v6 on v5

--- a/solution.py
+++ b/solution.py
@@ -285,8 +285,8 @@
 
     beside = [exists.astype(jnp.int32) for (dx, dk), exists in zip(ROUTES, there) if dx]
     pl.semaphore_wait(barrier, levs - 1 + sum(beside))
-    for i, exists in enumerate(there):
-        @pl.when(exists)
+    for i in (1, 2, 0, 4, 5, 3, 6, 7):
+        @pl.when(there[i])
         def _():
             halo_copy(i).start()
 

time: 26.7 us -> 26.4 us (0.989)
  Pallas kernels: 25.1 us -> 24.8 us
where the time goes in v6:
time: 26.4 us; the launch traced here: 26.3 us
  Pallas kernels  24.8 us (94%)
  local copies, waits for them, and re-layouts  1.47 us (6%)
    pallas_call x1, Pallas kernels, shards(): pl.pallas_call(lambda *refs: whole(tiles, levs, *refs), out_shape=jax.Sha...  24.8 us
    unnamed x1, local copies, waits for them, and re-layouts  1.47 us

profile of v6, /device:TPU:7, one launch (start us, length us, event | category | flops | bytes accessed | tf_op | source)
XLA Modules:
  0.0 26.3 jit_solution(5251560784704366889)
XLA Ops:
  0.0 24.8 %substeps_and_columns.1 = f32[128,128]{1,0:T(8,128)} custom-call(f32[128,128]{1,0:T(8,128)} %bitcast.12, f32[32,128]{1,0:T(8,128)} %bitcast.13, f32[32,128]{1,0:T(8,128)} %bitcast.14, f32[32,128]{1,0:T(8,128)} %bitcast.15, f32[32,128]{1,0:T(8,128)} %bitcast.16, f32[32,128]{1,0:T(8,128)} %bitcast.17, s32[4,128]{1,0:T(4,128)} %refs_6_.1, f32[1,8]{1,0:T(1,128)} %bitcast.21, ...), custom_call_target="tpu_custom_call" | custom-call | tf_op jit(solution)/shard_map/substeps_and_columns/pallas_call | solution.py:418
  24.8 1.5 %copy.19 = f32[4,8,4,128]{3,2,1,0:T(4,128)} copy(f32[4,8,4,128]{3,2,1,0:T(4,128)} %bitcast.11) | data formatting | bytes 131072

commit v7 on v6

--- a/solution.py
+++ b/solution.py
@@ -144,8 +144,10 @@
             p = jnp.exp2(s - jnp.max(s, axis=0, keepdims=True))
             p = p * (1.0 / jnp.sum(p, axis=0, keepdims=True)) * rs[...]
             probs.append(p)
-            z = [p * fm[i] for i in range(4)]
-            z = [a[0:8] + a[8:16] + a[16:24] + a[24:32] for a in z]
+            pb = p.astype(BF16)
+            z = [pb * fm[i].astype(BF16) for i in range(4)]
+            z = [(a[0:16] + a[16:32]).astype(F32) for a in z]
+            z = [a[0:8] + a[8:16] for a in z]
             for i in (0, 2):
                 sums.append(jnp.where(low, z[i], z[i + 1]) + pltpu.roll(jnp.where(low, z[i + 1], z[i]), 4, 0))
         parts.append(jnp.concatenate(probs + sums, axis=0).astype(BF16))
@@ -161,12 +163,12 @@
     ot[l0 + 1] = tend[:, 128:]
 
 
-def query_pairs(levels, fl, fm, bias, ls, lf, tcol, rk, rs, eq, ot, done=lambda n: None):
+def query_pairs(levels, fl, fm, bias, ls, lf, tcol, rk, rs, eq, ot, done=lambda n: None, early=()):
     pairs = len(levels)
     first, second = {}, {}
     for step in range(pairs + 2):
         if step < pairs:
-            first[step] = score_terms(levels[step], fl, ls)
+            first[step] = early[step] if step in early else score_terms(levels[step], fl, ls)
         if step >= 2:
             finish(levels[step - 2], second.pop(step - 2), lf, ot)
             done(step - 2)
@@ -362,6 +364,7 @@
         key_chunk(s * KL, KL // 2, fl, lk, rk, rs, eq)
 
     take(feat_s[lev], lev)
+    early = {12 + j: score_terms(lev * KL + 2 * j, fl, ls) for j in range(KL // 2)}
     for n, s in enumerate(peers):
         feature_copy(n).wait_recv()
         take(feat_r[s], s)
@@ -386,7 +389,7 @@
                 tendency_copy(turns[d]).start()
 
     query_pairs(
-        [to * KL + k for to in blocks for k in range(0, KL, 2)], fl, fm, bias, ls, lf, tcol, rk, rs, eq, ot, done
+        [to * KL + k for to in blocks for k in range(0, KL, 2)], fl, fm, bias, ls, lf, tcol, rk, rs, eq, ot, done, early
     )
     tend_r[lev] = tend_s[lev]
     for n in range(levs - 1):

time: 26.4 us -> 26.3 us (level)
  no operation moved by 1% of the time
where the time goes in v7:
time: 26.3 us; the launch traced here: 26.1 us
  Pallas kernels  24.6 us (94%)
  local copies, waits for them, and re-layouts  1.47 us (6%)
    pallas_call x1, Pallas kernels, shards(): pl.pallas_call(lambda *refs: whole(tiles, levs, *refs), out_shape=jax.Sha...  24.6 us
    unnamed x1, local copies, waits for them, and re-layouts  1.47 us

profile of v7, /device:TPU:7, one launch (start us, length us, event | category | flops | bytes accessed | tf_op | source)
XLA Modules:
  0.0 26.1 jit_solution(11871009210175996050)
XLA Ops:
  0.0 24.6 %substeps_and_columns.1 = f32[128,128]{1,0:T(8,128)} custom-call(f32[128,128]{1,0:T(8,128)} %bitcast.12, f32[32,128]{1,0:T(8,128)} %bitcast.13, f32[32,128]{1,0:T(8,128)} %bitcast.14, f32[32,128]{1,0:T(8,128)} %bitcast.15, f32[32,128]{1,0:T(8,128)} %bitcast.16, f32[32,128]{1,0:T(8,128)} %bitcast.17, s32[4,128]{1,0:T(4,128)} %refs_6_.1, f32[1,8]{1,0:T(1,128)} %bitcast.21, ...), custom_call_target="tpu_custom_call" | custom-call | tf_op jit(solution)/shard_map/substeps_and_columns/pallas_call | solution.py:421
  24.7 1.5 %copy.19 = f32[4,8,4,128]{3,2,1,0:T(4,128)} copy(f32[4,8,4,128]{3,2,1,0:T(4,128)} %bitcast.11) | data formatting | bytes 131072

commit v8 on v7

--- a/solution.py
+++ b/solution.py
@@ -131,6 +131,7 @@
 
 def attend(l0, x, out, fl, fm, bias, tcol, rk, rs, eq):
     parts = []
+    fb = [fm[i].astype(BF16) for i in range(4)]
     low = lax.broadcasted_iota(jnp.int32, (8, CELLS), 0) < 4
     for a in range(2):
         o = out[:, 128 * a : 128 * a + 128]
@@ -145,7 +146,7 @@
             p = p * (1.0 / jnp.sum(p, axis=0, keepdims=True)) * rs[...]
             probs.append(p)
             pb = p.astype(BF16)
-            z = [pb * fm[i].astype(BF16) for i in range(4)]
+            z = [pb * b for b in fb]
             z = [(a[0:16] + a[16:32]).astype(F32) for a in z]
             z = [a[0:8] + a[8:16] for a in z]
             for i in (0, 2):

time: 26.3 us -> 26.3 us (level)
  no operation moved by 1% of the time
where the time goes in v8:
time: 26.3 us; the launch traced here: 26.1 us
  Pallas kernels  24.6 us (94%)
  local copies, waits for them, and re-layouts  1.47 us (6%)
    pallas_call x1, Pallas kernels, shards(): pl.pallas_call(lambda *refs: whole(tiles, levs, *refs), out_shape=jax.Sha...  24.6 us
    unnamed x1, local copies, waits for them, and re-layouts  1.47 us

profile of v8, /device:TPU:7, one launch (start us, length us, event | category | flops | bytes accessed | tf_op | source)
XLA Modules:
  0.0 26.1 jit_solution(573490979150773722)
XLA Ops:
  0.0 24.6 %substeps_and_columns.1 = f32[128,128]{1,0:T(8,128)} custom-call(f32[128,128]{1,0:T(8,128)} %bitcast.12, f32[32,128]{1,0:T(8,128)} %bitcast.13, f32[32,128]{1,0:T(8,128)} %bitcast.14, f32[32,128]{1,0:T(8,128)} %bitcast.15, f32[32,128]{1,0:T(8,128)} %bitcast.16, f32[32,128]{1,0:T(8,128)} %bitcast.17, s32[4,128]{1,0:T(4,128)} %refs_6_.1, f32[1,8]{1,0:T(1,128)} %bitcast.21, ...), custom_call_target="tpu_custom_call" | custom-call | tf_op jit(solution)/shard_map/substeps_and_columns/pallas_call | solution.py:422
  24.6 1.5 %copy.19 = f32[4,8,4,128]{3,2,1,0:T(4,128)} copy(f32[4,8,4,128]{3,2,1,0:T(4,128)} %bitcast.11) | data formatting | bytes 131072
